TPU v7x, 128 devices: a whole 4x4x4 slice. The times are simulated.
128 devices in a mesh: sx: 16 (over x_hi, y, core), sy: 8 (over z, x_lo).
Axes of the slice: x: 4 (x_hi: 2, x_lo: 2; x = x_hi * 2 + x_lo), y: 4, z: 4, core: 2. Of those that a mesh axis runs over, the one named last changes fastest.
Arguments:
- coeffs: float32 [2, 16, 16, 8, 128, 128], P(None, 'sx', None, 'sy'), may hold values from -6 to 6
- deform: float32 [2, 4], replicated, may hold values from -0.08 to 0.08
Outputs:
- spectrum: float32 [2, 256, 1024, 128], P(None, 'sx', 'sy')
All inputs are finite; a program needn't handle non-finite values.
Results may differ from a plain program's by a relative error of at most 0.0014.
Values sent between devices are 32-bit elements; how exact they have to be, the bound alone decides.
No kernel may reach another device: no remote copies, remote signals or barrier semaphores. Data moves between devices by JAX's collectives and lax.ppermute only.
A program may use at most 64 MiB of HBM per device.

v0:
```python
import math

import jax
import jax.numpy as jnp
import numpy as np
from jax import lax
from jax.sharding import PartitionSpec as P

NODES = 4
RHS = 8


two_pi = 2.0 * math.pi
step_scale = math.sqrt(0.5)


def partner(value, axis, stride):
    return lax.ppermute(value, axis, [(i, i ^ 1 << stride) for i in range(lax.axis_size(axis))])


def cheb_nodes(count):
    return (1.0 - np.cos(np.pi * (2.0 * np.arange(count) + 1.0) / (2.0 * count))) / 2.0


def lagrange_table(count):
    nodes = cheb_nodes(count)
    table = np.ones((count, 2, count))
    for target_row in range(count):
        for sibling in range(2):
            spots = (sibling + nodes) / 2.0
            for other_node in range(count):
                if other_node != target_row:
                    table[target_row, sibling] = (
                        table[target_row, sibling]
                        * (spots - nodes[other_node])
                        / (nodes[target_row] - nodes[other_node])
                    )
    return table


def lane_matrix(weights, along, right_sides, count):
    ident_rhs = jnp.eye(right_sides, dtype=jnp.float32)
    ident_node = jnp.eye(count, dtype=jnp.float32)
    if along == 0:
        inner = jnp.kron(weights, ident_node)
    else:
        inner = jnp.kron(ident_node, weights)
    return jnp.kron(ident_rhs, inner)


def rotation(first_pos, second_pos, first_freq, second_freq, deform, scales):
    first_grid = (
        first_pos[:, None, None, None, :] + jnp.zeros_like(second_pos)[None, None, :, None, :]
    )
    second_grid = (
        second_pos[None, None, :, None, :] + jnp.zeros_like(first_pos)[:, None, None, None, :]
    )
    harmonic = jnp.arange(1, deform.shape[1] + 1).astype(jnp.float32) * math.pi
    summed = (first_grid + second_grid)[..., None] * harmonic
    differ = (first_grid - second_grid)[..., None] * harmonic
    first_warp = first_grid + jnp.sum(deform[0] * jnp.sin(summed), axis=-1)
    second_warp = second_grid + jnp.sum(deform[1] * jnp.sin(differ), axis=-1)
    angles = scales[0] * (first_warp * first_freq[None, :, None, None, None]) + scales[1] * (
        second_warp * second_freq[None, None, None, :, None]
    )
    return (jnp.cos(angles), jnp.sin(angles))


def orient(own_pos, other_pos, own_centre, other_centre, along, deform, scales):
    if along == 0:
        return rotation(own_pos, other_pos, own_centre, other_centre, deform, scales)
    return rotation(other_pos, own_pos, other_centre, own_centre, deform, scales)


def advance(
    children,
    parents,
    along,
    parent_count,
    other_boxes,
    other_count,
    parent_freq,
    freq_count,
    other_freq,
    other_fcount,
    deform,
    node_x,
    node_y,
    scales,
):
    own_nodes = node_x if along == 0 else node_y
    other_nodes = node_y if along == 0 else node_x
    other_pos = (other_boxes.astype(jnp.float32)[:, None] + other_nodes[None, :]) / other_count
    other_centre = (other_freq.astype(jnp.float32) + 0.5) / other_fcount
    parent_pos = (parents.astype(jnp.float32)[:, None] + own_nodes[None, :]) / parent_count
    pieces = []
    for freq_child in range(2):
        centre = ((2 * parent_freq + freq_child).astype(jnp.float32) + 0.5) / (2 * freq_count)
        total = None
        for member, boxes, matrix in children:
            child_pos = (boxes.astype(jnp.float32)[:, None] + own_nodes[None, :]) / (
                2 * parent_count
            )
            cosine, sine = orient(child_pos, other_pos, centre, other_centre, along, deform, scales)
            real_part = member[0] * cosine + member[1] * sine
            imag_part = member[1] * cosine - member[0] * sine
            rotated = jnp.stack([real_part, imag_part], axis=0)
            mixed = jnp.einsum(
                "zxfygn,mn->zxfygm", rotated, matrix, precision=lax.Precision.HIGHEST
            )
            total = mixed if total is None else total + mixed
        cosine, sine = orient(parent_pos, other_pos, centre, other_centre, along, deform, scales)
        out_real = (total[0] * cosine - total[1] * sine) * step_scale
        out_imag = (total[1] * cosine + total[0] * sine) * step_scale
        pieces.append(jnp.stack([out_real, out_imag], axis=0))
    if along == 0:
        joined = jnp.stack(pieces, axis=3)
        dims = joined.shape
        return joined.reshape(dims[:2] + (dims[2] * 2,) + dims[4:])
    joined = jnp.stack(pieces, axis=4)
    dims = joined.shape
    return joined.reshape(dims[:4] + (dims[4] * dims[5], dims[6]))


def natural_order(state, y_bits):
    dims = state.shape
    lowest = dims[4] >> y_bits
    folded = state.reshape((2, dims[2]) + (2,) * y_bits + (lowest, dims[5]))
    perm = [0, 1, 2 + y_bits] + [2 + (y_bits - 1 - level) for level in range(y_bits)] + [3 + y_bits]
    return jnp.transpose(folded, perm).reshape(2, dims[2], dims[4], dims[5])


def body(coeffs, deform):
    node_count = NODES
    right_sides = RHS
    lanes = coeffs.shape[5]
    freq_x = coeffs.shape[2]
    freq_y = coeffs.shape[4]
    lane_ids = np.arange(lanes)
    table = cheb_nodes(node_count)
    node_x = jnp.asarray(table[lane_ids // node_count % node_count], dtype=jnp.float32)
    node_y = jnp.asarray(table[lane_ids % node_count], dtype=jnp.float32)
    lagrange = jnp.asarray(lagrange_table(node_count), dtype=jnp.float32)
    x_devices = lax.axis_size("sx")
    y_devices = lax.axis_size("sy")
    scales = (two_pi * float(x_devices * freq_x), two_pi * float(y_devices * freq_y))
    x_bits = x_devices.bit_length() - 1
    y_bits = y_devices.bit_length() - 1
    x_index = lax.axis_index("sx")
    y_index = lax.axis_index("sy")
    pair_idx = jnp.arange(2)
    state = coeffs
    x_freq = jnp.arange(freq_x)
    y_freq = jnp.arange(freq_y)
    x_count = freq_x
    y_count = freq_y
    x_done = 0
    y_done = 0
    for depth in range(max(x_bits, y_bits)):
        flag = x_index >> depth & 1
        upper = 1 << x_bits - 1 - depth
        lower = freq_x // (2 * upper)
        split = state.reshape(2, 1, upper, 2, lower, 1, freq_y, lanes)
        half_shape = (2, 1, freq_x // 2, 1, freq_y, lanes)
        kept = lax.dynamic_index_in_dim(split, flag, 3, keepdims=False).reshape(half_shape)
        outgoing = lax.dynamic_index_in_dim(split, 1 - flag, 3, keepdims=False).reshape(half_shape)
        incoming = partner(outgoing, "sx", depth)
        parent_freq = lax.dynamic_index_in_dim(
            x_freq.reshape(upper, 2, lower), flag, 1, keepdims=False
        ).reshape(-1)
        own_box = jnp.reshape(x_index >> depth, (1,))
        partner_box = own_box ^ 1
        weights_own = lane_matrix(
            lax.dynamic_index_in_dim(lagrange, flag, 1, keepdims=False), 0, right_sides, node_count
        )
        weights_far = lane_matrix(
            lax.dynamic_index_in_dim(lagrange, 1 - flag, 1, keepdims=False),
            0,
            right_sides,
            node_count,
        )
        other_boxes = jnp.reshape(y_index >> y_done, (1,))
        children = [(kept, own_box, weights_own), (incoming, partner_box, weights_far)]
        state = advance(
            children,
            own_box >> 1,
            0,
            x_devices >> depth + 1,
            other_boxes,
            y_devices >> y_done,
            parent_freq,
            x_count,
            y_freq,
            y_count,
            deform,
            node_x,
            node_y,
            scales,
        )
        x_freq = (2 * parent_freq[:, None] + pair_idx[None, :]).reshape(-1)
        x_count = 2 * x_count
        x_done = depth + 1
        if depth < y_bits:
            flag = y_index >> depth & 1
            block = 1 << depth
            upper = 1 << y_bits - 1 - depth
            lowest = freq_y >> y_bits
            split = state.reshape(2, 1, freq_x, 1, block, upper, 2, lowest, lanes)
            half_shape = (2, 1, freq_x, 1, freq_y // 2, lanes)
            kept = lax.dynamic_index_in_dim(split, flag, 6, keepdims=False).reshape(half_shape)
            outgoing = lax.dynamic_index_in_dim(split, 1 - flag, 6, keepdims=False).reshape(
                half_shape
            )
            incoming = partner(outgoing, "sy", depth)
            parent_freq = lax.dynamic_index_in_dim(
                y_freq.reshape(block, upper, 2, lowest), flag, 2, keepdims=False
            ).reshape(-1)
            own_box = jnp.reshape(y_index >> depth, (1,))
            partner_box = own_box ^ 1
            weights_own = lane_matrix(
                lax.dynamic_index_in_dim(lagrange, flag, 1, keepdims=False),
                1,
                right_sides,
                node_count,
            )
            weights_far = lane_matrix(
                lax.dynamic_index_in_dim(lagrange, 1 - flag, 1, keepdims=False),
                1,
                right_sides,
                node_count,
            )
            other_boxes = jnp.reshape(x_index >> x_done, (1,))
            children = [(kept, own_box, weights_own), (incoming, partner_box, weights_far)]
            state = advance(
                children,
                own_box >> 1,
                1,
                y_devices >> depth + 1,
                other_boxes,
                x_devices >> x_done,
                parent_freq,
                y_count,
                x_freq,
                x_count,
                deform,
                node_x,
                node_y,
                scales,
            )
            y_freq = (2 * parent_freq[None, :] + pair_idx[:, None]).reshape(-1)
            y_count = 2 * y_count
            y_done = depth + 1
    return natural_order(state, y_bits)


def solution(mesh):
    placed = (P(None, "sx", None, "sy", None, None), P())
    return jax.shard_map(
        body, mesh=mesh, in_specs=placed, out_specs=P(None, "sx", "sy", None), check_vma=False
    )
```

profile of v0, /device:TPU:0, one launch (start us, length us, event | category | flops | bytes accessed | tf_op | source)
XLA Modules:
  0.0 274.1 jit_solution(7449510755625816798)
XLA Ops:
  0.0 2.3 dynamic-slice_bitcast_fusion.1
  18.3 3.1 %broadcast_multiply_fusion = (f32[8,16,8,16]{3,2,1,0:T(8,128)S(1)}, f32[8,16,8,16]{3,2,1,0:T(8,128)S(1)}, f32[8,16,8,16]{3,2,1,0:T(8,128)}, f32[8,16,8,16]{3,2,1...) fusion(f32[16,16]{1,0:T(8,128)} %mul.7215, ...), kind=kLoop, calls=%fused_computation.535 | loop fusion | flops 229376 | bytes 932096 | tf_op jit(solution)/shard_map/jit(kron)/mul | solution.py:48
  24.5 5.3 %fusion.354 = (f32[1,1,8,1,128,128]{5,4,2,0,3,1:T(8,128)S(1)}, f32[1,1,8,1,128,128]{5,4,2,0,3,1:T(8,128)S(1)}, f32[1,1,8,1,128,128]{5,4,2,0,3,1:T(8,128)S(1)}, f32[1,1,8,1,128,128]{5,4,2,0,3,1:T(8,128)S(1)}) fusion(f32[2,1,8,2,1,1,128,128]{7,6,3,2,0,5,4,1:T(8,128)} %bitcast.596, s32[]{:T(128)S(6)} %select_n.78, s32[]{:T(128)S(6)} %add.3301, ...), kind=kLoop, calls=%fused_computation.503 | loop fusion | flops 1835008 | bytes 3219464 | tf_op jit(solution)/shard_map/add | solution.py:105
  31.9 3.9 %fusion.352 = (f32[1,1,8,1,128,128]{5,4,2,0,3,1:T(8,128)S(1)}, f32[1,1,8,1,128,128]{5,4,2,0,3,1:T(8,128)S(1)}, f32[1,1,8,1,128,128]{5,4,2,0,3,1:T(8,128)S(1)}, f32[1,1,8,1,128,128]{5,4,2,0,3,1:T(8,128)S(1)}) fusion(f32[2,1,8,1,128,128]{5,4,2,0,3,1:T(8,128)S(1)} %collective-permute-done, f32[128,128]{1,0:T(8,128)S(1)} %copy-done.2, ...), kind=kLoop, calls=%fused_computation.501 | loop fusion | flops 1835008 | bytes 3219456 | tf_op jit(solution)/shard_map/add | solution.py:105
  39.8 4.0 %fusion.338 = (f32[1,1,8,1,128,128]{5,4,2,0,3,1:T(8,128)S(1)}, f32[1,1,8,1,128,128]{5,4,2,0,3,1:T(8,128)S(1)}, f32[1,1,8,1,128,128]{5,4,2,3,1,0:T(8,128)S(1)}) fusion(f32[2,8,128,128]{3,2,1,0:T(8,128)S(1)} %convolution_add_fusion.12, f32[8,128]{1,0:T(8,128)S(1)} %copy-done.33, f32[128,128]{1,0:T(8,128)S(1)} %get-tuple-element.385, ...), kind=kLoop, calls=%fused_computation.487 | loop fusion | flops 1835008 | bytes 3743744 | tf_op jit(solution)/shard_map/mul | solution.py:113
  51.0 4.4 %fusion.335 = (f32[1,1,16,1,64,128]{5,4,2,0,3,1:T(8,128)S(1)}, f32[1,1,16,1,64,128]{5,4,2,0,3,1:T(8,128)S(1)}, f32[1,1,16,1,64,128]{5,4,2,0,3,1:T(8,128)S(1)}, f32[1,1,16,1,64,128]{5,4,2,0,3,1:T(8,128)S(1)}) fusion(f32[1,1,16,1,64,128]{5,4,2,0,3,1:T(8,128)S(1)} %bitcast.597, f32[1,1,16,1,64,128]{5,4,2,0,3,1:T(8,128)S(1)} %bitcast.598, ...), kind=kLoop, calls=%fused_computation.484 | loop fusion | flops 1835008 | bytes 3219456 | tf_op jit(solution)/shard_map/add | solution.py:105
  57.4 13.9 %collective-permute-done.1 = f32[2,1,16,1,64,128]{5,4,2,0,3,1:T(8,128)} collective-permute-done((f32[2,1,16,1,64,128]{5,4,2,0,3,1:T(8,128)}, f32[2,1,16,1,64,128]{5,4,2,0,3,1:T(8,128)}, u32[]{:S(2)}, u32[]{:S(2)}) %collective-permute-start.1) | collective-permute-done | bytes 1048608 | tf_op jit(solution)/shard_map/ppermute | solution.py:18
  71.3 5.0 %fusion.333 = (f32[1,1,16,1,64,128]{5,4,2,0,3,1:T(8,128)S(1)}, f32[1,1,16,1,64,128]{5,4,2,0,3,1:T(8,128)S(1)}, f32[1,1,16,1,64,128]{5,4,2,0,3,1:T(8,128)S(1)}, f32[1,1,16,1,64,128]{5,4,2,0,3,1:T(8,128)S(1)}) fusion(f32[2,1,16,1,64,128]{5,4,2,0,3,1:T(8,128)} %collective-permute-done.1, f32[64,128]{1,0:T(8,128)S(1)} %copy-done.16, ...), kind=kLoop, calls=%fused_computation.482 | loop fusion | flops 1835008 | bytes 3219456 | tf_op jit(solution)/shard_map/add | solution.py:105
  80.3 3.9 %fusion.319 = (f32[1,1,16,1,64,128]{5,4,2,0,3,1:T(8,128)S(1)}, f32[1,1,16,1,64,128]{5,4,2,0,3,1:T(8,128)S(1)}, f32[1,1,16,1,64,128]{5,4,2,3,1,0:T(8,128)S(1)}) fusion(f32[2,16,64,128]{3,2,1,0:T(8,128)S(1)} %convolution_add_fusion.10, f32[64,128]{1,0:T(8,128)S(1)} %copy-done.15, f32[16,128]{1,0:T(8,128)S(1)} %get-tuple-element.376, ...), kind=kLoop, calls=%fused_computation.468 | loop fusion | flops 1835008 | bytes 3743744 | tf_op jit(solution)/shard_map/mul | solution.py:113
  90.3 4.8 %fusion.316 = (f32[1,1,8,1,128,128]{5,4,2,0,3,1:T(8,128)S(1)}, f32[1,1,8,1,128,128]{5,4,2,0,3,1:T(8,128)S(1)}, f32[1,1,8,1,128,128]{5,4,2,0,3,1:T(8,128)S(1)}, f32[1,1,8,1,128,128]{5,4,2,0,3,1:T(8,128)S(1)}) fusion(f32[1,1,8,1,128,128]{5,4,2,0,3,1:T(8,128)S(1)} %bitcast.599, f32[1,1,8,1,128,128]{5,4,2,0,3,1:T(8,128)S(1)} %bitcast.600, ...), kind=kLoop, calls=%fused_computation.465 | loop fusion | flops 1835008 | bytes 3219456 | tf_op jit(solution)/shard_map/add | solution.py:105
  97.2 13.9 %collective-permute-done.2 = f32[2,1,8,1,128,128]{5,4,2,0,3,1:T(8,128)} collective-permute-done((f32[2,1,8,1,128,128]{5,4,2,0,3,1:T(8,128)}, f32[2,1,8,1,128,128]{5,4,2,0,3,1:T(8,128)}, u32[]{:S(2)}, u32[]{:S(2)}) %collective-permute-start.2) | collective-permute-done | bytes 1048608 | tf_op jit(solution)/shard_map/ppermute | solution.py:18
  111.1 5.0 %fusion.314 = (f32[1,1,8,1,128,128]{5,4,2,0,3,1:T(8,128)S(1)}, f32[1,1,8,1,128,128]{5,4,2,0,3,1:T(8,128)S(1)}, f32[1,1,8,1,128,128]{5,4,2,0,3,1:T(8,128)S(1)}, f32[1,1,8,1,128,128]{5,4,2,0,3,1:T(8,128)S(1)}) fusion(f32[2,1,8,1,128,128]{5,4,2,0,3,1:T(8,128)} %collective-permute-done.2, f32[128,128]{1,0:T(8,128)S(1)} %copy-done.1, ...), kind=kLoop, calls=%fused_computation.463 | loop fusion | flops 1835008 | bytes 3219456 | tf_op jit(solution)/shard_map/add | solution.py:105
  118.0 4.0 %fusion.311 = (f32[1,1,8,1,128,128]{5,4,2,0,3,1:T(8,128)S(1)}, f32[1,1,8,1,128,128]{5,4,2,0,3,1:T(8,128)S(1)}, f32[1,1,8,1,128,128]{5,4,2,0,3,1:T(8,128)S(1)}, f32[1,1,8,1,128,128]{5,4,2,0,3,1:T(8,128)S(1)}) fusion(f32[2,8,128,128]{3,2,1,0:T(8,128)S(1)} %convolution_add_fusion.9, f32[128,128]{1,0:T(8,128)S(1)} %get-tuple-element.365, ...), kind=kLoop, calls=%fused_computation.460 | loop fusion | flops 2359296 | bytes 4268032 | tf_op jit(solution)/shard_map/mul | solution.py:113
  128.6 4.2 %fusion.300 = (f32[1,1,16,1,64,128]{5,4,2,0,3,1:T(8,128)S(1)}, f32[1,1,16,1,64,128]{5,4,2,0,3,1:T(8,128)S(1)}, f32[1,1,16,1,64,128]{5,4,2,0,3,1:T(8,128)S(1)}, f32[1,1,16,1,64,128]{5,4,2,0,3,1:T(8,128)S(1)}) fusion(f32[1,1,16,1,2,2,1,16,128]{8,7,6,5,4,2,0,3,1:T(8,128)S(1)} %get-tuple-element.70, ...), kind=kLoop, calls=%fused_computation.449 | loop fusion | flops 1835008 | bytes 3219456 | tf_op jit(solution)/shard_map/add | solution.py:105
  134.8 13.6 %collective-permute-done.3 = f32[2,1,16,1,64,128]{5,4,2,0,3,1:T(8,128)} collective-permute-done((f32[2,1,16,1,64,128]{5,4,2,0,3,1:T(8,128)}, f32[2,1,16,1,64,128]{5,4,2,0,3,1:T(8,128)}, u32[]{:S(2)}, u32[]{:S(2)}) %collective-permute-start.3) | collective-permute-done | bytes 1048608 | tf_op jit(solution)/shard_map/ppermute | solution.py:18
  148.3 5.0 %fusion.298 = (f32[1,1,16,1,64,128]{5,4,2,0,3,1:T(8,128)S(1)}, f32[1,1,16,1,64,128]{5,4,2,0,3,1:T(8,128)S(1)}, f32[1,1,16,1,64,128]{5,4,2,0,3,1:T(8,128)S(1)}, f32[1,1,16,1,64,128]{5,4,2,0,3,1:T(8,128)S(1)}) fusion(f32[2,1,16,1,64,128]{5,4,2,0,3,1:T(8,128)} %collective-permute-done.3, f32[64,128]{1,0:T(8,128)S(1)} %copy-done.11, ...), kind=kLoop, calls=%fused_computation.447 | loop fusion | flops 1835008 | bytes 3219456 | tf_op jit(solution)/shard_map/add | solution.py:105
  155.3 4.0 %fusion.295 = (f32[1,1,16,1,64,128]{5,4,2,0,3,1:T(8,128)S(1)}, f32[1,1,16,1,64,128]{5,4,2,0,3,1:T(8,128)S(1)}, f32[1,1,16,1,64,128]{5,4,2,0,3,1:T(8,128)S(1)}, f32[1,1,16,1,64,128]{5,4,2,0,3,1:T(8,128)S(1)}) fusion(f32[2,16,64,128]{3,2,1,0:T(8,128)S(1)} %convolution_add_fusion.7, f32[64,128]{1,0:T(8,128)S(1)} %copy-done.9, ...), kind=kLoop, calls=%fused_computation.444 | loop fusion | flops 2359296 | bytes 4268032 | tf_op jit(solution)/shard_map/mul | solution.py:113
  161.1 3.1 %collective-permute-start.4 = (f32[2,1,8,1,128,128]{5,4,2,0,3,1:T(8,128)}, f32[2,1,8,1,128,128]{5,4,2,0,3,1:T(8,128)}, u32[]{:S(2)}, u32[]{:S(2)}) collective-permute-start(f32[2,1,8,1,128,128]{5,4,2,0,3,1:T(8,128)} %bitcast.105), channel_id=1, source_target_pairs={{0,32},{8,40},{16,48},{24,56},{32,0},{40,8},{48,16},{56,24},{64,96... | collective-permute-start | bytes 3145736 | tf_op jit(solution)/shard_map/ppermute | solution.py:18
  166.9 4.3 %fusion.284 = (f32[1,1,8,1,128,128]{5,4,2,0,3,1:T(8,128)S(1)}, f32[1,1,8,1,128,128]{5,4,2,0,3,1:T(8,128)S(1)}, f32[1,1,8,1,128,128]{5,4,2,0,3,1:T(8,128)S(1)}, f32[1,1,8,1,128,128]{5,4,2,0,3,1:T(8,128)S(1)}) fusion(f32[1,1,8,1,128,128]{5,4,2,0,3,1:T(8,128)S(1)} %bitcast.601, f32[1,1,8,1,128,128]{5,4,2,0,3,1:T(8,128)S(1)} %bitcast.602, ...), kind=kLoop, calls=%fused_computation.433 | loop fusion | flops 1835008 | bytes 3219456 | tf_op jit(solution)/shard_map/add | solution.py:105
  173.2 12.9 %collective-permute-done.4 = f32[2,1,8,1,128,128]{5,4,2,0,3,1:T(8,128)} collective-permute-done((f32[2,1,8,1,128,128]{5,4,2,0,3,1:T(8,128)}, f32[2,1,8,1,128,128]{5,4,2,0,3,1:T(8,128)}, u32[]{:S(2)}, u32[]{:S(2)}) %collective-permute-start.4) | collective-permute-done | bytes 1048608 | tf_op jit(solution)/shard_map/ppermute | solution.py:18
  186.1 5.0 %fusion.282 = (f32[1,1,8,1,128,128]{5,4,2,0,3,1:T(8,128)S(1)}, f32[1,1,8,1,128,128]{5,4,2,0,3,1:T(8,128)S(1)}, f32[1,1,8,1,128,128]{5,4,2,0,3,1:T(8,128)S(1)}, f32[1,1,8,1,128,128]{5,4,2,0,3,1:T(8,128)S(1)}) fusion(f32[2,1,8,1,128,128]{5,4,2,0,3,1:T(8,128)} %collective-permute-done.4, f32[128,128]{1,0:T(8,128)S(1)} %get-tuple-element.344, ...), kind=kLoop, calls=%fused_computation.431 | loop fusion | flops 1835008 | bytes 3219456 | tf_op jit(solution)/shard_map/add | solution.py:105
  193.1 4.0 %fusion.279 = (f32[1,1,8,1,128,128]{5,4,2,0,3,1:T(8,128)S(1)}, f32[1,1,8,1,128,128]{5,4,2,0,3,1:T(8,128)S(1)}, f32[1,1,8,1,128,128]{5,4,2,0,3,1:T(8,128)S(1)}, f32[1,1,8,1,128,128]{5,4,2,0,3,1:T(8,128)S(1)}) fusion(f32[2,8,128,128]{3,2,1,0:T(8,128)S(1)} %convolution_add_fusion.5, f32[128,128]{1,0:T(8,128)S(1)} %get-tuple-element.343, ...), kind=kLoop, calls=%fused_computation.428 | loop fusion | flops 2359296 | bytes 4268032 | tf_op jit(solution)/shard_map/mul | solution.py:113
  198.9 3.4 %collective-permute-start.5 = (f32[2,1,16,1,64,128]{5,4,2,0,3,1:T(8,128)}, f32[2,1,16,1,64,128]{5,4,2,0,3,1:T(8,128)}, u32[]{:S(2)}, u32[]{:S(2)}) collective-permute-start(f32[2,1,16,1,64,128]{5,4,2,0,3,1:T(8,128)} %bitcast.129), channel_id=1, source_target_pairs={{0,4},{1,5},{2,6},{3,7},{4,0},{5,1},{6,2},{7,3},{8,12},{9,13},{10,... | collective-permute-start | bytes 3145736 | tf_op jit(solution)/shard_map/ppermute | solution.py:18
  205.0 4.1 %fusion.268 = (f32[1,1,16,1,64,128]{5,4,2,0,3,1:T(8,128)S(1)}, f32[1,1,16,1,64,128]{5,4,2,0,3,1:T(8,128)S(1)}, f32[1,1,16,1,64,128]{5,4,2,0,3,1:T(8,128)S(1)}, f32[1,1,16,1,64,128]{5,4,2,0,3,1:T(8,128)S(1)}) fusion(f32[1,1,16,1,64,128]{5,4,2,0,3,1:T(8,128)S(1)} %bitcast.603, f32[1,1,16,1,64,128]{5,4,2,0,3,1:T(8,128)S(1)} %bitcast.604, ...), kind=kLoop, calls=%fused_computation.417 | loop fusion | flops 1835008 | bytes 3219456 | tf_op jit(solution)/shard_map/add | solution.py:105
  211.0 12.0 %collective-permute-done.5 = f32[2,1,16,1,64,128]{5,4,2,0,3,1:T(8,128)} collective-permute-done((f32[2,1,16,1,64,128]{5,4,2,0,3,1:T(8,128)}, f32[2,1,16,1,64,128]{5,4,2,0,3,1:T(8,128)}, u32[]{:S(2)}, u32[]{:S(2)}) %collective-permute-start.5) | collective-permute-done | bytes 1048608 | tf_op jit(solution)/shard_map/ppermute | solution.py:18
  223.1 5.0 %fusion.266 = (f32[1,1,16,1,64,128]{5,4,2,0,3,1:T(8,128)S(1)}, f32[1,1,16,1,64,128]{5,4,2,0,3,1:T(8,128)S(1)}, f32[1,1,16,1,64,128]{5,4,2,0,3,1:T(8,128)S(1)}, f32[1,1,16,1,64,128]{5,4,2,0,3,1:T(8,128)S(1)}) fusion(f32[2,1,16,1,64,128]{5,4,2,0,3,1:T(8,128)} %collective-permute-done.5, f32[64,128]{1,0:T(8,128)S(1)} %copy-done.5, ...), kind=kLoop, calls=%fused_computation.415 | loop fusion | flops 1835008 | bytes 3219456 | tf_op jit(solution)/shard_map/add | solution.py:105
  230.0 4.0 %fusion.263 = (f32[1,1,16,1,64,128]{5,4,2,0,3,1:T(8,128)S(1)}, f32[1,1,16,1,64,128]{5,4,2,0,3,1:T(8,128)S(1)}, f32[1,1,16,1,64,128]{5,4,2,0,3,1:T(8,128)S(1)}, f32[1,1,16,1,64,128]{5,4,2,0,3,1:T(8,128)S(1)}) fusion(f32[2,16,64,128]{3,2,1,0:T(8,128)S(1)} %convolution_add_fusion.3, f32[64,128]{1,0:T(8,128)S(1)} %get-tuple-element.324, ...), kind=kLoop, calls=%fused_computation.412 | loop fusion | flops 2359296 | bytes 4268032 | tf_op jit(solution)/shard_map/mul | solution.py:113
  235.8 2.9 %collective-permute-start.6 = (f32[2,1,8,1,128,128]{5,4,2,0,3,1:T(8,128)}, f32[2,1,8,1,128,128]{5,4,2,0,3,1:T(8,128)}, u32[]{:S(2)}, u32[]{:S(2)}) collective-permute-start(f32[2,1,8,1,128,128]{5,4,2,0,3,1:T(8,128)} %dynamic-slice_bitcast_fusion), channel_id=1, source_target_pairs={{0,64},{8,72},{16,80},{24,88},{32,96},{40,104},{48,112},{56,120},{... | collective-permute-start | bytes 3145736 | tf_op jit(solution)/shard_map/ppermute | solution.py:18
  239.3 4.1 %fusion.252 = (f32[1,1,8,1,128,128]{5,4,2,0,3,1:T(8,128)S(1)}, f32[1,1,8,1,128,128]{5,4,2,0,3,1:T(8,128)S(1)}, f32[1,1,8,1,128,128]{5,4,2,0,3,1:T(8,128)S(1)}, f32[1,1,8,1,128,128]{5,4,2,0,3,1:T(8,128)S(1)}) fusion(f32[2,1,1,2,8,1,128,128]{7,6,4,5,3,2,1,0:T(8,128)S(1)} %bitcast.582, s32[]{:T(128)S(6)} %select_n.90, s32[]{:T(128)S(6)} %add.3301, ...), kind=kLoop, calls=%fused_computation.401 | loop fusion | flops 1835008 | bytes 3219464 | tf_op jit(solution)/shard_map/add | solution.py:105
  245.4 13.6 %collective-permute-done.6 = f32[2,1,8,1,128,128]{5,4,2,0,3,1:T(8,128)} collective-permute-done((f32[2,1,8,1,128,128]{5,4,2,0,3,1:T(8,128)}, f32[2,1,8,1,128,128]{5,4,2,0,3,1:T(8,128)}, u32[]{:S(2)}, u32[]{:S(2)}) %collective-permute-start.6) | collective-permute-done | bytes 1048608 | tf_op jit(solution)/shard_map/ppermute | solution.py:18
  259.0 5.0 %fusion.250 = (f32[1,1,8,1,128,128]{5,4,2,0,3,1:T(8,128)S(1)}, f32[1,1,8,1,128,128]{5,4,2,0,3,1:T(8,128)S(1)}, f32[1,1,8,1,128,128]{5,4,2,0,3,1:T(8,128)S(1)}, f32[1,1,8,1,128,128]{5,4,2,0,3,1:T(8,128)S(1)}) fusion(f32[2,1,8,1,128,128]{5,4,2,0,3,1:T(8,128)} %collective-permute-done.6, f32[128,128]{1,0:T(8,128)S(1)} %get-tuple-element.280, ...), kind=kLoop, calls=%fused_computation.399 | loop fusion | flops 1835008 | bytes 3219456 | tf_op jit(solution)/shard_map/add | solution.py:105
  266.0 4.0 %fusion.247 = (f32[1,1,8,1,128,128]{5,4,2,0,3,1:T(8,128)S(1)}, f32[1,1,8,1,128,128]{5,4,2,0,3,1:T(8,128)S(1)}, f32[1,1,8,1,128,128]{5,4,2,0,3,1:T(8,128)S(1)}, f32[1,1,8,1,128,128]{5,4,2,0,3,1:T(8,128)S(1)}) fusion(f32[2,8,128,128]{3,2,1,0:T(8,128)S(1)} %convolution_add_fusion.1, f32[128,128]{1,0:T(8,128)S(1)} %get-tuple-element.279, ...), kind=kLoop, calls=%fused_computation.396 | loop fusion | flops 2359296 | bytes 4268032 | tf_op jit(solution)/shard_map/mul | solution.py:113
  (311 shorter events, 84.9 us)
Async XLA Ops:
  0.0 9.0 %copy-start.42 = (f32[128]{0:T(128)S(1)}, f32[128]{0:T(128)}, u32[]{:S(2)}) copy-start(f32[128]{0:T(128)} %constant.243.clone) | copy-start | bytes 1540
  0.0 9.0 %copy-start.43 = (f32[128]{0:T(128)S(1)}, f32[128]{0:T(128)}, u32[]{:S(2)}) copy-start(f32[128]{0:T(128)} %constant.244.clone) | copy-start | bytes 1540
  0.0 4.6 %copy-start.59 = (f32[2,4]{1,0:T(2,128)S(1)}, f32[2,4]{1,0:T(2,128)}, u32[]{:S(2)}) copy-start(f32[2,4]{1,0:T(2,128)} %param.6) | copy-start | bytes 100
  2.3 29.5 %collective-permute-start = (f32[2,1,8,1,128,128]{5,4,2,0,3,1:T(8,128)}, f32[2,1,8,1,128,128]{5,4,2,0,3,1:T(8,128)S(1)}, u32[]{:S(2)}, u32[]{:S(2)}) collective-permute-start(f32[2,1,8,1,128,128]{5,4,2,0,3,1:T(8,128)} %dynamic-slice_bitcast_fusion.1), channel_id=1, source_target_pairs={{0,8},{8,0},{16,24},{24,16},{32,40},{40,32},{48,56},{56,48},{64,72... | collective-permute-start | bytes 3145736 | tf_op jit(solution)/shard_map/ppermute | solution.py:18
  45.5 25.9 %collective-permute-start.1 = (f32[2,1,16,1,64,128]{5,4,2,0,3,1:T(8,128)}, f32[2,1,16,1,64,128]{5,4,2,0,3,1:T(8,128)}, u32[]{:S(2)}, u32[]{:S(2)}) collective-permute-start(f32[2,1,16,1,64,128]{5,4,2,0,3,1:T(8,128)} %bitcast.34), channel_id=1, source_target_pairs={{0,1},{1,0},{2,3},{3,2},{4,5},{5,4},{6,7},{7,6},{8,9},{9,8},{10,11... | collective-permute-start | bytes 3145736 | tf_op jit(solution)/shard_map/ppermute | solution.py:18
  55.4 16.0 %copy-start.16 = (f32[64,128]{1,0:T(8,128)S(1)}, f32[64,128]{1,0:T(8,128)}, u32[]{:S(2)}) copy-start(f32[64,128]{1,0:T(8,128)} %get-tuple-element.369) | copy-start | bytes 98308
  55.4 16.0 %copy-start.17 = (f32[64,128]{1,0:T(8,128)S(1)}, f32[64,128]{1,0:T(8,128)}, u32[]{:S(2)}) copy-start(f32[64,128]{1,0:T(8,128)} %get-tuple-element.370) | copy-start | bytes 98308
  85.9 25.1 %collective-permute-start.2 = (f32[2,1,8,1,128,128]{5,4,2,0,3,1:T(8,128)}, f32[2,1,8,1,128,128]{5,4,2,0,3,1:T(8,128)}, u32[]{:S(2)}, u32[]{:S(2)}) collective-permute-start(f32[2,1,8,1,128,128]{5,4,2,0,3,1:T(8,128)} %bitcast.59), channel_id=1, source_target_pairs={{0,16},{8,24},{16,0},{24,8},{32,48},{40,56},{48,32},{56,40},{64,80... | collective-permute-start | bytes 3145736 | tf_op jit(solution)/shard_map/ppermute | solution.py:18
  95.2 15.9 %copy-start.1 = (f32[128,128]{1,0:T(8,128)S(1)}, f32[128,128]{1,0:T(8,128)}, u32[]{:S(2)}) copy-start(f32[128,128]{1,0:T(8,128)} %get-tuple-element.366) | copy-start | bytes 196612
  95.2 15.9 %copy-start.29 = (f32[8,128]{1,0:T(8,128)S(1)}, f32[8,128]{1,0:T(8,128)}, u32[]{:S(2)}) copy-start(f32[8,128]{1,0:T(8,128)} %get-tuple-element.358) | copy-start | bytes 12292
  95.2 15.9 %copy-start.30 = (f32[8,128]{1,0:T(8,128)S(1)}, f32[8,128]{1,0:T(8,128)}, u32[]{:S(2)}) copy-start(f32[8,128]{1,0:T(8,128)} %get-tuple-element.359) | copy-start | bytes 12292
  123.8 4.7 %copy-start.13 = (f32[64,128]{1,0:T(8,128)S(1)}, f32[64,128]{1,0:T(8,128)}, u32[]{:S(2)}) copy-start(f32[64,128]{1,0:T(8,128)} %get-tuple-element.350) | copy-start | bytes 98308
  123.8 4.7 %copy-start.14 = (f32[64,128]{1,0:T(8,128)S(1)}, f32[64,128]{1,0:T(8,128)}, u32[]{:S(2)}) copy-start(f32[64,128]{1,0:T(8,128)} %get-tuple-element.351) | copy-start | bytes 98308
  123.8 24.5 %collective-permute-start.3 = (f32[2,1,16,1,64,128]{5,4,2,0,3,1:T(8,128)}, f32[2,1,16,1,64,128]{5,4,2,0,3,1:T(8,128)}, u32[]{:S(2)}, u32[]{:S(2)}) collective-permute-start(f32[2,1,16,1,64,128]{5,4,2,0,3,1:T(8,128)} %bitcast.82), channel_id=1, source_target_pairs={{0,2},{1,3},{2,0},{3,1},{4,6},{5,7},{6,4},{7,5},{8,10},{9,11},{10,... | collective-permute-start | bytes 3145736 | tf_op jit(solution)/shard_map/ppermute | solution.py:18
  132.7 15.6 %copy-start.11 = (f32[64,128]{1,0:T(8,128)S(1)}, f32[64,128]{1,0:T(8,128)}, u32[]{:S(2)}) copy-start(f32[64,128]{1,0:T(8,128)} %get-tuple-element.347) | copy-start | bytes 98308
  132.8 15.6 %copy-start.12 = (f32[64,128]{1,0:T(8,128)S(1)}, f32[64,128]{1,0:T(8,128)}, u32[]{:S(2)}) copy-start(f32[64,128]{1,0:T(8,128)} %get-tuple-element.348) | copy-start | bytes 98308
  161.0 5.8 %copy-start = (f32[128,128]{1,0:T(8,128)S(1)}, f32[128,128]{1,0:T(8,128)}, u32[]{:S(2)}) copy-start(f32[128,128]{1,0:T(8,128)} %get-tuple-element.345) | copy-start | bytes 196612
  161.0 5.8 %copy-start.27 = (f32[8,128]{1,0:T(8,128)S(1)}, f32[8,128]{1,0:T(8,128)}, u32[]{:S(2)}) copy-start(f32[8,128]{1,0:T(8,128)} %get-tuple-element.339) | copy-start | bytes 12292
  161.0 5.8 %copy-start.28 = (f32[8,128]{1,0:T(8,128)S(1)}, f32[8,128]{1,0:T(8,128)}, u32[]{:S(2)}) copy-start(f32[8,128]{1,0:T(8,128)} %get-tuple-element.340) | copy-start | bytes 12292
  161.1 25.1 %collective-permute-start.4 = (f32[2,1,8,1,128,128]{5,4,2,0,3,1:T(8,128)}, f32[2,1,8,1,128,128]{5,4,2,0,3,1:T(8,128)}, u32[]{:S(2)}, u32[]{:S(2)}) collective-permute-start(f32[2,1,8,1,128,128]{5,4,2,0,3,1:T(8,128)} %bitcast.105), channel_id=1, source_target_pairs={{0,32},{8,40},{16,48},{24,56},{32,0},{40,8},{48,16},{56,24},{64,96... | collective-permute-start | bytes 3145736 | tf_op jit(solution)/shard_map/ppermute | solution.py:18
  171.2 14.9 %copy-start.25 = (f32[8,128]{1,0:T(8,128)S(1)}, f32[8,128]{1,0:T(8,128)}, u32[]{:S(2)}) copy-start(f32[8,128]{1,0:T(8,128)} %get-tuple-element.336) | copy-start | bytes 12292
  171.2 14.9 %copy-start.26 = (f32[8,128]{1,0:T(8,128)S(1)}, f32[8,128]{1,0:T(8,128)}, u32[]{:S(2)}) copy-start(f32[8,128]{1,0:T(8,128)} %get-tuple-element.337) | copy-start | bytes 12292
  198.9 6.0 %copy-start.7 = (f32[64,128]{1,0:T(8,128)S(1)}, f32[64,128]{1,0:T(8,128)}, u32[]{:S(2)}) copy-start(f32[64,128]{1,0:T(8,128)} %get-tuple-element.328) | copy-start | bytes 98308
  198.9 6.1 %copy-start.8 = (f32[64,128]{1,0:T(8,128)S(1)}, f32[64,128]{1,0:T(8,128)}, u32[]{:S(2)}) copy-start(f32[64,128]{1,0:T(8,128)} %get-tuple-element.329) | copy-start | bytes 98308
  198.9 24.2 %collective-permute-start.5 = (f32[2,1,16,1,64,128]{5,4,2,0,3,1:T(8,128)}, f32[2,1,16,1,64,128]{5,4,2,0,3,1:T(8,128)}, u32[]{:S(2)}, u32[]{:S(2)}) collective-permute-start(f32[2,1,16,1,64,128]{5,4,2,0,3,1:T(8,128)} %bitcast.129), channel_id=1, source_target_pairs={{0,4},{1,5},{2,6},{3,7},{4,0},{5,1},{6,2},{7,3},{8,12},{9,13},{10,... | collective-permute-start | bytes 3145736 | tf_op jit(solution)/shard_map/ppermute | solution.py:18
  209.0 14.0 %copy-start.5 = (f32[64,128]{1,0:T(8,128)S(1)}, f32[64,128]{1,0:T(8,128)}, u32[]{:S(2)}) copy-start(f32[64,128]{1,0:T(8,128)} %get-tuple-element.325) | copy-start | bytes 98308
  209.0 14.0 %copy-start.6 = (f32[64,128]{1,0:T(8,128)S(1)}, f32[64,128]{1,0:T(8,128)}, u32[]{:S(2)}) copy-start(f32[64,128]{1,0:T(8,128)} %get-tuple-element.326) | copy-start | bytes 98308
  234.7 4.5 %copy-start.23 = (f32[8,128]{1,0:T(8,128)S(1)}, f32[8,128]{1,0:T(8,128)}, u32[]{:S(2)}) copy-start(f32[8,128]{1,0:T(8,128)} %get-tuple-element.277) | copy-start | bytes 12292
  234.7 4.5 %copy-start.24 = (f32[8,128]{1,0:T(8,128)S(1)}, f32[8,128]{1,0:T(8,128)}, u32[]{:S(2)}) copy-start(f32[8,128]{1,0:T(8,128)} %get-tuple-element.278) | copy-start | bytes 12292
  235.8 23.2 %collective-permute-start.6 = (f32[2,1,8,1,128,128]{5,4,2,0,3,1:T(8,128)}, f32[2,1,8,1,128,128]{5,4,2,0,3,1:T(8,128)}, u32[]{:S(2)}, u32[]{:S(2)}) collective-permute-start(f32[2,1,8,1,128,128]{5,4,2,0,3,1:T(8,128)} %dynamic-slice_bitcast_fusion), channel_id=1, source_target_pairs={{0,64},{8,72},{16,80},{24,88},{32,96},{40,104},{48,112},{56,120},{... | collective-permute-start | bytes 3145736 | tf_op jit(solution)/shard_map/ppermute | solution.py:18
  243.4 15.7 %copy-start.21 = (f32[8,128]{1,0:T(8,128)S(1)}, f32[8,128]{1,0:T(8,128)}, u32[]{:S(2)}) copy-start(f32[8,128]{1,0:T(8,128)} %get-tuple-element.274) | copy-start | bytes 12292
  243.4 15.7 %copy-start.22 = (f32[8,128]{1,0:T(8,128)S(1)}, f32[8,128]{1,0:T(8,128)}, u32[]{:S(2)}) copy-start(f32[8,128]{1,0:T(8,128)} %get-tuple-element.275) | copy-start | bytes 12292
  (39 other events, 98.2 us)
where the time goes:
time: 278 us; the launch traced here: 274 us
  other arithmetic  116 us (42%)
  waiting for transfers between devices  80 us (29%)
  local copies, waits for them, and re-layouts  34.4 us (12%)
  matrix products  27.6 us (10%)
  starting transfers between devices  14.6 us (5%)
    ppermute x7, waiting for transfers between devices, partner(): lax.ppermute(value, axis, [(i, i ^ 1 << stride) for i in range(lax.axis_s...  80 us
    add x14, other arithmetic, advance(): real_part = member[0] * cosine + member[1] * sine  64.7 us
    mul x7, other arithmetic, advance(): out_real = (total[0] * cosine - total[1] * sine) * step_scale  27.9 us
    dot_general x28, matrix products, advance(): jnp.einsum('zxfygn,mn->zxfygm', rotated, matrix, precision=lax.Precision....  27.6 us
    ppermute x7, starting transfers between devices, partner(): lax.ppermute(value, axis, [(i, i ^ 1 << stride) for i in range(lax.axis_s...  14.6 us
    mul x14, local copies, waits for them, and re-layouts, lane_matrix(): return jnp.kron(ident_rhs, inner)  13 us
  transfers between devices with their start and end apart: 7, of which 6 were waited for; matrix products, arithmetic and copies ran while one was open for 30% of the time, Pallas kernels for 0%

commit v1 on v0

v1 whole, which is shorter than its diff:
```python
import math

import jax
import jax.numpy as jnp
import numpy as np
from jax import lax
from jax.experimental import pallas as pl
from jax.experimental.pallas import tpu as pltpu
from jax.sharding import PartitionSpec as P

NODES = 4
RHS = 8
POINTS = NODES * NODES
LANES = RHS * POINTS
MIB = 1 << 20


def cheb_nodes(count):
    return (1.0 - np.cos(np.pi * (2.0 * np.arange(count) + 1.0) / (2.0 * count))) / 2.0


def lagrange_table(count):
    nodes = cheb_nodes(count)
    table = np.ones((count, 2, count))
    for row in range(count):
        for sibling in range(2):
            spots = (sibling + nodes) / 2.0
            for other in range(count):
                if other != row:
                    table[row, sibling] *= (spots - nodes[other]) / (nodes[row] - nodes[other])
    return table


def pattern_x():
    L, e2, e4, one = lagrange_table(NODES), np.eye(2), np.eye(NODES), np.ones((2, 2))
    return np.einsum("hH,yY,zZ,asu,vV->hyzavHsYZuV", e2, e2, one, L, e4).reshape(128, 256)


def pattern_y():
    L, e2, e4, one = lagrange_table(NODES), np.eye(2), np.eye(NODES), np.ones((2, 2))
    return np.einsum("hH,zZ,aA,bsv->hzabHsZAv", e2, one, e4, L).reshape(64, 128)


def pattern_x_last():
    L, e4, one = lagrange_table(NODES), np.eye(NODES), np.ones((2, 2))
    return np.einsum("zZ,asu,bB->zabsZuB", one, L, e4).reshape(32, 64)


def pattern_y_first():
    L, e2, e4, one = lagrange_table(NODES), np.eye(2), np.eye(NODES), np.ones((2, 2))
    return np.einsum("gG,hH,zZ,uU,bsv->ghzubGHsZUv", e4, e2, one, e4, L).reshape(256, 512)


def columns(dims, first, second, first_turns, second_turns):
    names, sizes = zip(*dims)
    grid = dict(zip(names, np.meshgrid(*[np.arange(s) for s in sizes], indexing="ij")))
    shape = grid["z"].shape
    flat = lambda v: np.broadcast_to(v, shape).reshape(-1)
    return np.stack(
        [flat(first(grid)), flat(second(grid)), flat(first_turns), flat(second_turns), flat(grid["z"])]
    )


def column_tables():
    q = cheb_nodes(NODES)
    groups = []
    for gx in range(4):
        for gy in range(4):
            one = columns(
                [("h", 2), ("l", 2), ("y", 2), ("z", 2), ("u", 4), ("v", 4)],
                lambda g: (4 * gx + 2 * g["h"] + g["l"] + q[g["u"]]) / 16,
                lambda g: (2 * gy + g["y"] + q[g["v"]]) / 8,
                4.0,
                0.0,
            )
            two = columns(
                [("h", 2), ("y", 2), ("z", 2), ("u", 4), ("v", 4)],
                lambda g: (2 * gx + g["h"] + q[g["u"]]) / 8,
                lambda g: (2 * gy + g["y"] + q[g["v"]]) / 8,
                0.0,
                2.0,
            )
            three = columns(
                [("h", 2), ("z", 2), ("u", 4), ("v", 4)],
                lambda g: (2 * gx + g["h"] + q[g["u"]]) / 8,
                lambda g: (gy + q[g["v"]]) / 4,
                2.0,
                0.0,
            )
            groups.append(np.concatenate([one, two, three, np.zeros((5, 64))], axis=1))
    inner = np.stack(groups, axis=1)
    four = columns(
        [("g", 4), ("h", 2), ("l", 2), ("z", 2), ("u", 4), ("v", 4)],
        lambda g: (g["g"] + q[g["u"]]) / 4,
        lambda g: (2 * g["h"] + g["l"] + q[g["v"]]) / 4,
        0.0,
        1.0,
    )
    five = columns(
        [("h", 2), ("l", 2), ("y", 2), ("z", 2), ("u", 4), ("v", 4)],
        lambda g: (2 * g["h"] + g["l"] + q[g["u"]]) / 4,
        lambda g: (g["y"] + q[g["v"]]) / 2,
        1.0,
        0.0,
    )
    six = columns(
        [("h", 2), ("y", 2), ("z", 2), ("u", 4), ("v", 4)],
        lambda g: (g["h"] + q[g["u"]]) / 2,
        lambda g: (g["y"] + q[g["v"]]) / 2,
        0.0,
        0.5,
    )
    seven = columns(
        [("h", 2), ("z", 2), ("u", 4), ("v", 4)],
        lambda g: (g["h"] + q[g["u"]]) / 2,
        lambda g: q[g["v"]] + 0.0 * g["h"],
        0.5,
        0.0,
    )
    outer = np.concatenate([four, five, six, seven, np.zeros((5, 64))], axis=1)
    outer = np.broadcast_to(outer[:, None], (5, 8, 1024))
    return inner.astype(np.float32), outer.astype(np.float32)


def lane_nodes():
    lane = np.arange(LANES)
    q = cheb_nodes(NODES)
    both = np.stack([q[lane // NODES % NODES], q[lane % NODES]])
    return np.broadcast_to(both[:, None], (2, 8, LANES)).astype(np.float32)


SINE = [
    (-1) ** k * (2.0 * math.pi) ** (2 * k + 1) / math.factorial(2 * k + 1) for k in range(7)
]


def sine_quarter(x):
    square = x * x
    total = jnp.full_like(x, SINE[-1])
    for coefficient in SINE[-2::-1]:
        total = total * square + coefficient
    return total * x


def turn(x):
    part = x - jnp.round(x)
    size = jnp.abs(part)
    folded = jnp.where(size > 0.25, jnp.where(part > 0, 0.5, -0.5) - part, part)
    return sine_quarter(0.25 - size), sine_quarter(folded)


def sine(x):
    part = x - jnp.round(x)
    folded = jnp.where(jnp.abs(part) > 0.25, jnp.where(part > 0, 0.5, -0.5) - part, part)
    return sine_quarter(folded)


def warp(deform, first, second):
    total, differ = 0.5 * (first + second), 0.5 * (first - second)
    y1, y2 = None, None
    for m in range(4):
        one = deform[0, m] * sine(total * (m + 1.0))
        two = deform[1, m] * sine(differ * (m + 1.0))
        y1 = one if y1 is None else y1 + one
        y2 = two if y2 is None else y2 + two
    return first + y1, second + y2


def exchange(values, lane):
    width = values[0].shape[-1]
    for bit in range(3):
        step = 1 << bit
        low = (lane & step) == 0
        new = list(values)
        for i in range(8):
            if not i & step:
                a, b = values[i], values[i | step]
                new[i] = jnp.where(low, a, pltpu.roll(b, step, 1))
                new[i | step] = jnp.where(low, pltpu.roll(a, width - step, 1), b)
        values = new
    return values


def split(x):
    high = x.astype(jnp.bfloat16)
    low = (x - high.astype(jnp.float32)).astype(jnp.bfloat16)
    return high, low


def iota(shape, dim):
    return lax.broadcasted_iota(jnp.int32, shape, dim)


PRE_BOXES = 4


def pre_kernel(deform, nodes, coeffs, out, first_cos, first_sin, second_cos, second_sin):
    step = pl.program_id(0)

    @pl.when(step == 0)
    def _():
        sx = lax.axis_index("sx").astype(jnp.float32)
        sy = lax.axis_index("sy").astype(jnp.float32)
        y1, y2 = warp(deform, (nodes[0] + sx) * (1 / 16), (nodes[1] + sy) * (1 / 8))
        y1, y2 = y1[0:1] * 16.0, y2[0:1] * 8.0
        box = iota((16, LANES), 0).astype(jnp.float32) + 0.5
        c, s = turn(y1 * box)
        first_cos[...] = c
        first_sin[...] = s
        row = iota((128, LANES), 0)
        box = ((row & 7) * 16 + (row >> 3)).astype(jnp.float32) + 0.5
        c, s = turn(y2 * box)
        second_cos[...] = c
        second_sin[...] = s

    lane = iota((16, LANES), 1)

    def one(j, carry):
        b1 = step * PRE_BOXES + j
        c1, s1 = first_cos[pl.ds(b1, 1), :], first_sin[pl.ds(b1, 1), :]
        c2, s2 = second_cos[...], second_sin[...]
        c = c1 * c2 - s1 * s2
        s = s1 * c2 + c1 * s2
        both = [
            jnp.concatenate(
                [coeffs[z, 0, j, 0, pl.ds(f, 8, stride=16), :] for f in range(16)], axis=0
            )
            for z in range(2)
        ]
        rotated = (both[0] * c + both[1] * s, both[1] * c - both[0] * s)
        for z in range(2):
            flipped = rotated[z].T
            pieces = exchange([flipped[16 * r : 16 * r + 16] for r in range(8)], lane)
            for k in range(8):
                out[j * 8 + k, pl.ds(16 * z, 16), :] = pieces[k]
        return carry

    lax.fori_loop(0, PRE_BOXES, one, 0)


def pre(coeffs, deform):
    smem = pl.BlockSpec(memory_space=pltpu.SMEM)
    return pl.pallas_call(
        pre_kernel,
        grid=(16 // PRE_BOXES,),
        out_shape=jax.ShapeDtypeStruct((128, 32, 128), jnp.float32),
        in_specs=[
            smem,
            pl.BlockSpec((2, 8, LANES), lambda i: (0, 0, 0)),
            pl.BlockSpec((2, 1, PRE_BOXES, 1, 128, LANES), lambda i: (0, 0, i, 0, 0, 0)),
        ],
        out_specs=pl.BlockSpec((8 * PRE_BOXES, 32, LANES), lambda i: (i, 0, 0)),
        scratch_shapes=[
            pltpu.VMEM((16, LANES), jnp.float32),
            pltpu.VMEM((16, LANES), jnp.float32),
            pltpu.VMEM((128, LANES), jnp.float32),
            pltpu.VMEM((128, LANES), jnp.float32),
        ],
        cost_estimate=pl.CostEstimate(
            flops=10 * MIB, bytes_accessed=4 * MIB, transcendentals=0
        ),
    )(deform, jnp.asarray(lane_nodes()), coeffs)


def phase_rows(tables, deform, store):
    y1, y2 = warp(deform, tables[0], tables[1])
    c, s = turn(tables[2] * y1 + tables[3] * y2)
    real = tables[4] < 0.5
    for child in range(2):
        sine_part = s if child else -s
        store[child, 0] = jnp.where(real, c, sine_part)
        store[child, 1] = jnp.where(real, -sine_part, c)


def dot(a, b):
    return jnp.dot(a, b, precision=lax.Precision.HIGHEST, preferred_element_type=jnp.float32)


def level(pattern, rows, child, part):
    shape = pattern.shape
    real = (iota(shape, 0) & POINTS) == 0
    return pattern * jnp.where(real, rows[child][0][:, part], rows[child][1][:, part])


def build_kernel(
    deform, nodes, inner, outer, wide, px, py, px_last, m1, m2, first, second, rows_in, rows_out
):
    phase_rows(inner, deform, rows_in)
    phase_rows(outer, deform, rows_out)

    def chain(rows, at_x, at_y, at_last):
        last = jnp.concatenate(
            [level(px_last[...], rows, c, slice(at_last, at_last + 64)) for c in range(2)], axis=0
        )
        parts = [dot(last, level(py[...], rows, c, slice(at_y, at_y + 128))) for c in range(2)]
        joined = jnp.concatenate(
            [parts[cy][32 * cx : 32 * cx + 32] for cx in range(2) for cy in range(2)], axis=0
        )
        return [
            dot(joined, level(px[...], rows, c, slice(at_x, at_x + 256))) for c in range(2)
        ]

    def group(g, carry):
        rows = [[rows_in[c, z, pl.ds(g, 1), :] for z in range(2)] for c in range(2)]
        for c, value in enumerate(chain(rows, 0, 256, 384)):
            high, low = split(value)
            m1[g, pl.ds(128 * c, 128), :] = high
            m1[g, pl.ds(256 + 128 * c, 128), :] = low
        return carry

    lax.fori_loop(0, 16, group, 0)

    rows = [[rows_out[c, z, 0:1, :] for z in range(2)] for c in range(2)]
    for c5, value in enumerate(chain(rows, 512, 768, 896)):
        for c4 in range(2):
            block = dot(value, level(wide[...], rows, c4, slice(0, 512)))
            for c7 in range(2):
                for c6 in range(2):
                    high, low = split(block[64 * c7 + 32 * c6 : 64 * c7 + 32 * c6 + 32])
                    at = 32 * (8 * c5 + 4 * c7 + 2 * c4 + c6)
                    m2[0, pl.ds(at, 32), :] = high
                    m2[1, pl.ds(at, 32), :] = low

    sx = lax.axis_index("sx").astype(jnp.float32)
    sy = lax.axis_index("sy").astype(jnp.float32)
    y1, y2 = warp(deform, nodes[0], nodes[1])
    c, s = turn(y1[0:1] * (iota((16, LANES), 0).astype(jnp.float32) + (16.0 * sx + 0.5)))
    scale = math.sqrt(0.5) ** 7
    first[0] = c * scale
    first[1] = s * scale
    c, s = turn(y2[0:1] * (iota((128, LANES), 0).astype(jnp.float32) + (128.0 * sy + 0.5)))
    second[0] = c
    second[1] = s


def build(deform):
    inner, outer = column_tables()
    consts = [lane_nodes(), inner, outer, pattern_y_first(), pattern_x(), pattern_y(), pattern_x_last()]
    vmem = pl.BlockSpec(memory_space=pltpu.VMEM)
    return pl.pallas_call(
        build_kernel,
        out_shape=[
            jax.ShapeDtypeStruct((16, 512, 256), jnp.bfloat16),
            jax.ShapeDtypeStruct((2, 512, 512), jnp.bfloat16),
            jax.ShapeDtypeStruct((2, 16, LANES), jnp.float32),
            jax.ShapeDtypeStruct((2, 128, LANES), jnp.float32),
        ],
        in_specs=[pl.BlockSpec(memory_space=pltpu.SMEM)] + [vmem] * 7,
        out_specs=[vmem] * 4,
        scratch_shapes=[
            pltpu.VMEM((2, 2, 16, 512), jnp.float32),
            pltpu.VMEM((2, 2, 8, 1024), jnp.float32),
        ],
        compiler_params=pltpu.CompilerParams(vmem_limit_bytes=32 * MIB),
        cost_estimate=pl.CostEstimate(
            flops=6000 * MIB, bytes_accessed=40 * MIB, transcendentals=0
        ),
    )(deform, *[jnp.asarray(c, dtype=jnp.float32) for c in consts])


def mul(a, b):
    return jnp.dot(a, b, preferred_element_type=jnp.float32)


def post_kernel(m1, m2, first, second, got, out, high, low, acc, done, sems):
    def stage_one(g, carry):
        gx, gy = g // 4, g % 4
        x = jnp.concatenate(
            [got[pl.ds((4 * gx + i) * 8 + 2 * gy, 2)].reshape(64, LANES) for i in range(4)], axis=0
        )
        xh, xl = split(x)
        res = mul(m1[g], jnp.concatenate([xh, xl], axis=1))
        res = res[:256, :128] + (res[:256, 128:] + res[256:, :128])
        yh, yl = split(res)
        for c13 in range(4):
            for c2 in range(2):
                piece = slice(64 * c13 + 32 * c2, 64 * c13 + 32 * c2 + 32)
                at = pl.ds(pl.multiple_of(32 * g, 32), 32)
                high[c13, at, pl.ds(128 * c2, 128)] = yh[piece]
                low[c13, at, pl.ds(128 * c2, 128)] = yl[piece]
        return carry

    lax.fori_loop(0, 16, stage_one, 0)

    lane = iota((16, LANES), 1)

    def copies(c13):
        return [
            pltpu.make_async_copy(
                done.at[z, pl.ds(4 * c13, 4)], out.at[z, pl.ds(4 * c13, 4)], sems.at[z, c13]
            )
            for z in range(2)
        ]

    for c13 in range(4):
        acc[...] = mul(m2[0], high[c13]) + (mul(m2[0], low[c13]) + mul(m2[1], high[c13]))

        def finish(c57, carry):
            cx = 4 * c13 + c57
            c1, s1 = first[0, pl.ds(cx, 1), :], first[1, pl.ds(cx, 1), :]
            c2, s2 = second[0], second[1]
            c = c1 * c2 - s1 * s2
            s = s1 * c2 + c1 * s2
            turned = []
            for z in range(2):
                pieces = []
                for cy in range(8):
                    top, rest = cy >> 2, cy & 3
                    at = pl.multiple_of(128 * c57, 128) + 32 * rest + 16 * z
                    pieces.append(acc[pl.ds(at, 16), pl.ds(128 * top, 128)])
                turned.append(jnp.concatenate(exchange(pieces, lane), axis=0).T)
            done[0, cx] = turned[0] * c - turned[1] * s
            done[1, cx] = turned[1] * c + turned[0] * s
            return carry

        lax.fori_loop(0, 4, finish, 0)
        for copy in copies(c13):
            copy.start()
    for c13 in range(4):
        for copy in copies(c13):
            copy.wait()


def post(m1, m2, first, second, got):
    vmem = pl.BlockSpec(memory_space=pltpu.VMEM)
    return pl.pallas_call(
        post_kernel,
        out_shape=jax.ShapeDtypeStruct((2, 16, 128, LANES), jnp.float32),
        in_specs=[vmem] * 5,
        out_specs=pl.BlockSpec(memory_space=pl.ANY),
        scratch_shapes=[
            pltpu.VMEM((4, 512, 256), jnp.bfloat16),
            pltpu.VMEM((4, 512, 256), jnp.bfloat16),
            pltpu.VMEM((512, 256), jnp.float32),
            pltpu.VMEM((2, 16, 128, LANES), jnp.float32),
            pltpu.SemaphoreType.DMA((2, 4)),
        ],
        compiler_params=pltpu.CompilerParams(vmem_limit_bytes=32 * MIB),
        cost_estimate=pl.CostEstimate(
            flops=4000 * MIB, bytes_accessed=10 * MIB, transcendentals=0
        ),
    )(m1, m2, first, second, got)


def body(coeffs, deform):
    sent = pre(coeffs, deform)
    got = lax.all_to_all(sent, ("sx", "sy"), 0, 0, tiled=True)
    return post(*build(deform), got)


def solution(mesh):
    placed = (P(None, "sx", None, "sy", None, None), P())
    return jax.shard_map(
        body, mesh=mesh, in_specs=placed, out_specs=P(None, "sx", "sy", None), check_vma=False
    )
```

time: 278 us -> 66.5 us (0.24); the launches traced: 274 us -> 66.3 us
  other arithmetic: 116 us -> 0 us
  waiting for transfers between devices: 80 us -> 15.5 us
  Pallas kernels: 0 us -> 33.1 us
  local copies, waits for them, and re-layouts: 34.4 us -> 6.37 us
  matrix products: 27.6 us -> 0 us
  starting transfers between devices: 14.6 us -> 11.1 us
    ppermute x7 -> x0, waiting for transfers between devices: 80 us -> none  [partner(): lax.ppermute(value, axis, [(i, i ^ 1 << stride) for i in range(lax.axis_s...]
    add x19 -> x0, other arithmetic: 66.5 us -> none  [the longest x14 64.7 us: advance(): real_part = member[0] * cosine + member[1] * sine]
    mul x33 -> x0, other arithmetic: 44.7 us -> none  [the longest x7 27.9 us: advance(): out_real = (total[0] * cosine - total[1] * sine) * step_scale]
    pallas_call x0 -> x3, Pallas kernels: none -> 33.1 us  [the longest x1 14.1 us: post(): pl.pallas_call(post_kernel, out_shape=jax.ShapeDtypeStruct((2, 16, 128, L...]
    dot_general x28 -> x0, matrix products: 27.6 us -> none  [advance(): jnp.einsum('zxfygn,mn->zxfygm', rotated, matrix, precision=lax.Precision....]
    mul x40 -> x0, local copies, waits for them, and re-layouts: 16.6 us -> none  [the longest x14 13 us: lane_matrix(): return jnp.kron(ident_rhs, inner)]
    all_to_all x0 -> x1, waiting for transfers between devices: none -> 15.5 us  [body(): got = lax.all_to_all(sent, ('sx', 'sy'), 0, 0, tiled=True)]
    ppermute x7 -> x0, starting transfers between devices: 14.6 us -> none  [partner(): lax.ppermute(value, axis, [(i, i ^ 1 << stride) for i in range(lax.axis_s...]
  transfers between devices with their start and end apart: 7 -> 1, of which waited for: 6 -> 1; matrix products, arithmetic and copies ran while one was open for 30% -> 0% of each run, Pallas kernels for 0% -> 17%
where the time goes in v1:
time: 66.5 us; the launch traced here: 66.3 us
  Pallas kernels  33.1 us (50%)
  waiting for transfers between devices  15.5 us (23%)
  starting transfers between devices  11.1 us (17%)
  local copies, waits for them, and re-layouts  6.37 us (10%)
    all_to_all x1, waiting for transfers between devices, body(): got = lax.all_to_all(sent, ('sx', 'sy'), 0, 0, tiled=True)  15.5 us
    pallas_call x1, Pallas kernels, post(): pl.pallas_call(post_kernel, out_shape=jax.ShapeDtypeStruct((2, 16, 128, L...  14.1 us
    pallas_call x1, Pallas kernels, build(): pl.pallas_call(build_kernel, out_shape=[jax.ShapeDtypeStruct((16, 512, 25...  11.4 us
    all_to_all x1, starting transfers between devices, body(): got = lax.all_to_all(sent, ('sx', 'sy'), 0, 0, tiled=True)  11.1 us
    pallas_call x1, Pallas kernels, pre(): pl.pallas_call(pre_kernel, grid=(16 // PRE_BOXES,), out_shape=jax.ShapeDt...  7.62 us
    unnamed x24, local copies, waits for them, and re-layouts  6.37 us
  transfers between devices with their start and end apart: 1, of which 1 were waited for; matrix products, arithmetic and copies ran while one was open for 0% of the time, Pallas kernels for 17%

profile of v1, /device:TPU:0, one launch (start us, length us, event | category | flops | bytes accessed | tf_op | source)
XLA Modules:
  0.0 66.3 jit_solution(17826311303743092409)
XLA Ops:
  0.0 7.6 %shard_map.101 = f32[128,32,128]{2,1,0:T(8,128)} custom-call(f32[2,4]{1,0:T(2,128)} %deform.3, f32[2,8,128]{2,1,0:T(8,128)} %constant.14.clone.nodes, f32[2,1,16,1,128,128]{5,4,3,2,1,0:T(8,128)} %coeffs.1), custom_call_target="tpu_custom_call" | custom-call | flops 10485760 | bytes 4194304 | tf_op jit(solution)/shard_map/pallas_call | solution.py:243
  7.6 0.0 copy-start
  7.6 0.0 copy-start.1
  7.6 0.0 copy-start.2
  7.6 0.0 copy-start.3
  7.6 0.0 copy-start.4
  7.7 0.0 copy-start.5
  7.7 0.0 copy-start.6
  7.7 0.0 copy-start.7
  7.7 11.1 %all-to-all-start = ((f32[128,32,128]{2,1,0:T(8,128)}), f32[128,32,128]{2,1,0:T(8,128)S(1)}, u32[]{:S(2)}, u32[]{:S(2)}) async-start(f32[128,32,128]{2,1,0:T(8,128)} %shard_map.101), calls=%async_computation | async-start | bytes 4194304 | tf_op jit(solution)/shard_map/all_to_all | solution.py:447
  18.8 0.0 copy-done
  18.9 0.0 copy-done.1
  18.9 0.0 copy-done.2
  18.9 0.0 copy-done.3
  18.9 0.0 copy-done.4
  18.9 0.0 copy-done.5
  18.9 0.0 copy-done.6
  18.9 0.0 copy-done.7
  18.9 11.4 %shard_map.100 = (bf16[16,512,256]{2,1,0:T(8,128)(2,1)S(1)}, bf16[2,512,512]{2,1,0:T(8,128)(2,1)S(1)}, f32[2,16,128]{2,1,0:T(8,128)S(1)}, f32[2,128,128]{2,1,0:T(8,128)S(1)}) custom-call(f32[2,4]{1,0:T(2,128)S(1)} %copy-done.1, f32[2,8,128]{2,1,0:T(8,128)S(1)} %copy-done, f32[5,16,512]{2,1,0:T(8,128)S(1)} %copy-done.4, f32[5,8,1024]{2,1,0:T(8,128)S(1)} %copy-done.3, ...), custom_call_target="tpu_custom_call" | custom-call | flops 6291456000 | bytes 41943040 | tf_op jit(solution)/shard_map/pallas_call | solution.py:340
  30.3 0.0 copy-start.8
  30.3 1.9 %copy-done.8 = bf16[16,512,256]{2,1,0:T(8,128)(2,1)} copy-done((bf16[16,512,256]{2,1,0:T(8,128)(2,1)}, bf16[16,512,256]{2,1,0:T(8,128)(2,1)S(1)}, u32[]{:S(2)}) %copy-start.8) | copy-done | bytes 4194328
  32.3 0.0 copy-start.10
  32.3 1.0 %copy-done.10 = bf16[2,512,512]{2,1,0:T(8,128)(2,1)} copy-done((bf16[2,512,512]{2,1,0:T(8,128)(2,1)}, bf16[2,512,512]{2,1,0:T(8,128)(2,1)S(1)}, u32[]{:S(2)}) %copy-start.10) | copy-done | bytes 1048600
  33.2 15.5 %all-to-all-done.got = f32[128,32,128]{2,1,0:T(8,128)S(1)} async-done(((f32[128,32,128]{2,1,0:T(8,128)}), f32[128,32,128]{2,1,0:T(8,128)S(1)}, u32[]{:S(2)}, u32[]{:S(2)}) %all-to-all-start) | async-done | bytes 2097184 | tf_op jit(solution)/shard_map/all_to_all | solution.py:447
  48.8 0.0 copy-start.9
  48.8 2.2 %copy-done.9 = bf16[16,512,256]{2,1,0:T(8,128)(2,1)S(1)} copy-done((bf16[16,512,256]{2,1,0:T(8,128)(2,1)S(1)}, bf16[16,512,256]{2,1,0:T(8,128)(2,1)}, u32[]{:S(2)}) %copy-start.9) | copy-done | bytes 4194328
  51.0 0.0 copy-start.11
  51.0 1.2 %copy-done.11 = bf16[2,512,512]{2,1,0:T(8,128)(2,1)S(1)} copy-done((bf16[2,512,512]{2,1,0:T(8,128)(2,1)S(1)}, bf16[2,512,512]{2,1,0:T(8,128)(2,1)}, u32[]{:S(2)}) %copy-start.11) | copy-done | bytes 1048600
  52.2 14.1 %shard_map.102 = f32[2,16,128,128]{3,2,1,0:T(8,128)} custom-call(bf16[16,512,256]{2,1,0:T(8,128)(2,1)S(1)} %copy-done.9, bf16[2,512,512]{2,1,0:T(8,128)(2,1)S(1)} %copy-done.11, f32[2,16,128]{2,1,0:T(8,128)S(1)} %get-tuple-element.11.first, f32[2,128,128]{2,1,0:T(8,128)S(1)} %get-tuple-element.12.second, f32[128,32,128]{2,1,0:T(8,128)S(1)} %all-to-all-done.got), custom_call_target="tpu_custom_call" | custom-call | flops 4194304000 | bytes 10485760 | tf_op jit(solution)/shard_map/pallas_call | solution.py:426
Async XLA Ops:
  7.6 11.2 %copy-start = (f32[2,8,128]{2,1,0:T(8,128)S(1)}, f32[2,8,128]{2,1,0:T(8,128)}, u32[]{:S(2)}) copy-start(f32[2,8,128]{2,1,0:T(8,128)} %constant.14.clone.nodes) | copy-start | bytes 24580
  7.6 11.2 %copy-start.1 = (f32[2,4]{1,0:T(2,128)S(1)}, f32[2,4]{1,0:T(2,128)}, u32[]{:S(2)}) copy-start(f32[2,4]{1,0:T(2,128)} %deform.3) | copy-start | bytes 100
  7.6 11.2 %copy-start.2 = (f32[256,512]{1,0:T(8,128)S(1)}, f32[256,512]{1,0:T(8,128)}, u32[]{:S(2)}) copy-start(f32[256,512]{1,0:T(8,128)} %constant.17.clone.wide) | copy-start | bytes 1572868
  7.6 11.3 %copy-start.3 = (f32[5,8,1024]{2,1,0:T(8,128)S(1)}, f32[5,8,1024]{2,1,0:T(8,128)}, u32[]{:S(2)}) copy-start(f32[5,8,1024]{2,1,0:T(8,128)} %constant.16.clone.outer) | copy-start | bytes 491524
  7.6 11.2 %copy-start.4 = (f32[5,16,512]{2,1,0:T(8,128)S(1)}, f32[5,16,512]{2,1,0:T(8,128)}, u32[]{:S(2)}) copy-start(f32[5,16,512]{2,1,0:T(8,128)} %constant.15.clone.inner) | copy-start | bytes 491524
  7.7 11.2 %copy-start.5 = (f32[128,256]{1,0:T(8,128)S(1)}, f32[128,256]{1,0:T(8,128)}, u32[]{:S(2)}) copy-start(f32[128,256]{1,0:T(8,128)} %constant.18.clone.px) | copy-start | bytes 393220
  7.7 11.2 %copy-start.6 = (f32[64,128]{1,0:T(8,128)S(1)}, f32[64,128]{1,0:T(8,128)}, u32[]{:S(2)}) copy-start(f32[64,128]{1,0:T(8,128)} %constant.19.clone.py) | copy-start | bytes 98308
  7.7 11.2 %copy-start.7 = (f32[32,64]{1,0:T(8,128)S(1)}, f32[32,64]{1,0:T(8,128)}, u32[]{:S(2)}) copy-start(f32[32,64]{1,0:T(8,128)} %constant.20.clone.px_last) | copy-start | bytes 24580
  7.7 41.1 %all-to-all-start = ((f32[128,32,128]{2,1,0:T(8,128)}), f32[128,32,128]{2,1,0:T(8,128)S(1)}, u32[]{:S(2)}, u32[]{:S(2)}) async-start(f32[128,32,128]{2,1,0:T(8,128)} %shard_map.101), calls=%async_computation | async-start | bytes 4194304 | tf_op jit(solution)/shard_map/all_to_all | solution.py:447
  30.3 1.9 %copy-start.8 = (bf16[16,512,256]{2,1,0:T(8,128)(2,1)}, bf16[16,512,256]{2,1,0:T(8,128)(2,1)S(1)}, u32[]{:S(2)}) copy-start(bf16[16,512,256]{2,1,0:T(8,128)(2,1)S(1)} %get-tuple-element.9.m1) | copy-start | bytes 12582916
  32.3 1.0 %copy-start.10 = (bf16[2,512,512]{2,1,0:T(8,128)(2,1)}, bf16[2,512,512]{2,1,0:T(8,128)(2,1)S(1)}, u32[]{:S(2)}) copy-start(bf16[2,512,512]{2,1,0:T(8,128)(2,1)S(1)} %get-tuple-element.10.m2) | copy-start | bytes 3145732
  48.8 2.2 %copy-start.9 = (bf16[16,512,256]{2,1,0:T(8,128)(2,1)S(1)}, bf16[16,512,256]{2,1,0:T(8,128)(2,1)}, u32[]{:S(2)}) copy-start(bf16[16,512,256]{2,1,0:T(8,128)(2,1)} %copy-done.8) | copy-start | bytes 12582916
  51.0 1.2 %copy-start.11 = (bf16[2,512,512]{2,1,0:T(8,128)(2,1)S(1)}, bf16[2,512,512]{2,1,0:T(8,128)(2,1)}, u32[]{:S(2)}) copy-start(bf16[2,512,512]{2,1,0:T(8,128)(2,1)} %copy-done.10) | copy-start | bytes 3145732

commit v2 on v1

--- a/solution.py
+++ b/solution.py
@@ -122,13 +122,6 @@
     return inner.astype(np.float32), outer.astype(np.float32)
 
 
-def lane_nodes():
-    lane = np.arange(LANES)
-    q = cheb_nodes(NODES)
-    both = np.stack([q[lane // NODES % NODES], q[lane % NODES]])
-    return np.broadcast_to(both[:, None], (2, 8, LANES)).astype(np.float32)
-
-
 SINE = [
     (-1) ** k * (2.0 * math.pi) ** (2 * k + 1) / math.factorial(2 * k + 1) for k in range(7)
 ]
@@ -166,19 +159,26 @@
     return first + y1, second + y2
 
 
-def exchange(values, lane):
-    width = values[0].shape[-1]
-    for bit in range(3):
-        step = 1 << bit
-        low = (lane & step) == 0
-        new = list(values)
-        for i in range(8):
-            if not i & step:
-                a, b = values[i], values[i | step]
-                new[i] = jnp.where(low, a, pltpu.roll(b, step, 1))
-                new[i | step] = jnp.where(low, pltpu.roll(a, width - step, 1), b)
-        values = new
-    return values
+def flip_maps():
+    row, lane = iota((8, LANES), 0), iota((8, LANES), 1)
+    spot = lane & 15
+    back, on = row - spot, row + spot
+    lanes = [(lane & ~15) | ((back + 8 * half) & 15) for half in range(2)]
+    return back & 7, (back & 8) == 0, lanes, on & 7, (on & 8) == 0
+
+
+def flip(low, high, maps):
+    rows, first, lanes, rows_back, first_back = maps
+
+    def spread(x, y, rows, first):
+        x = jnp.take_along_axis(x, rows, axis=0)
+        y = jnp.take_along_axis(y, rows, axis=0)
+        return jnp.where(first, x, y), jnp.where(first, y, x)
+
+    low, high = spread(low, high, rows, first)
+    low = jnp.take_along_axis(low, lanes[0], axis=1)
+    high = jnp.take_along_axis(high, lanes[1], axis=1)
+    return spread(low, high, rows_back, first_back)
 
 
 def split(x):
@@ -187,79 +187,98 @@
     return high, low
 
 
+def lane_nodes():
+    lane = iota((8, LANES), 1)
+    q = [float(v) for v in cheb_nodes(NODES)]
+
+    def pick(t):
+        return jnp.where(t < 2, jnp.where(t == 0, q[0], q[1]), jnp.where(t == 2, q[2], q[3]))
+
+    return pick((lane >> 2) & 3), pick(lane & 3)
+
+
 def iota(shape, dim):
     return lax.broadcasted_iota(jnp.int32, shape, dim)
 
 
-PRE_BOXES = 4
-
-
-def pre_kernel(deform, nodes, coeffs, out, first_cos, first_sin, second_cos, second_sin):
-    step = pl.program_id(0)
-
-    @pl.when(step == 0)
-    def _():
-        sx = lax.axis_index("sx").astype(jnp.float32)
-        sy = lax.axis_index("sy").astype(jnp.float32)
-        y1, y2 = warp(deform, (nodes[0] + sx) * (1 / 16), (nodes[1] + sy) * (1 / 8))
-        y1, y2 = y1[0:1] * 16.0, y2[0:1] * 8.0
-        box = iota((16, LANES), 0).astype(jnp.float32) + 0.5
-        c, s = turn(y1 * box)
-        first_cos[...] = c
-        first_sin[...] = s
-        row = iota((128, LANES), 0)
-        box = ((row & 7) * 16 + (row >> 3)).astype(jnp.float32) + 0.5
-        c, s = turn(y2 * box)
-        second_cos[...] = c
-        second_sin[...] = s
-
-    lane = iota((16, LANES), 1)
-
-    def one(j, carry):
-        b1 = step * PRE_BOXES + j
+PARTS = 4
+BOXES = 16 // PARTS
+
+
+def pre_kernel(deform, coeffs, out, held, ready, first_cos, first_sin, second_cos, second_sin, sems, out_sems):
+    copies = [
+        pltpu.make_async_copy(
+            coeffs.at[:, 0, pl.ds(BOXES * p, BOXES), 0], held.at[:, pl.ds(BOXES * p, BOXES)], sems.at[p]
+        )
+        for p in range(PARTS)
+    ]
+    sends = [
+        pltpu.make_async_copy(
+            ready.at[pl.ds(8 * BOXES * p, 8 * BOXES)], out.at[pl.ds(8 * BOXES * p, 8 * BOXES)], out_sems.at[p]
+        )
+        for p in range(PARTS)
+    ]
+    for copy in copies:
+        copy.start()
+
+    nodes = lane_nodes()
+    sx = lax.axis_index("sx").astype(jnp.float32)
+    sy = lax.axis_index("sy").astype(jnp.float32)
+    y1, y2 = warp(deform, (nodes[0] + sx) * (1 / 16), (nodes[1] + sy) * (1 / 8))
+    y1, y2 = y1[0:1] * 16.0, y2[0:1] * 8.0
+    first_cos[...], first_sin[...] = turn(y1 * (iota((16, LANES), 0).astype(jnp.float32) + 0.5))
+    second_cos[...], second_sin[...] = turn(y2 * (iota((128, LANES), 0).astype(jnp.float32) + 0.5))
+    maps = flip_maps()
+
+    def one(b1, carry):
         c1, s1 = first_cos[pl.ds(b1, 1), :], first_sin[pl.ds(b1, 1), :]
-        c2, s2 = second_cos[...], second_sin[...]
-        c = c1 * c2 - s1 * s2
-        s = s1 * c2 + c1 * s2
-        both = [
-            jnp.concatenate(
-                [coeffs[z, 0, j, 0, pl.ds(f, 8, stride=16), :] for f in range(16)], axis=0
-            )
-            for z in range(2)
-        ]
-        rotated = (both[0] * c + both[1] * s, both[1] * c - both[0] * s)
-        for z in range(2):
-            flipped = rotated[z].T
-            pieces = exchange([flipped[16 * r : 16 * r + 16] for r in range(8)], lane)
-            for k in range(8):
-                out[j * 8 + k, pl.ds(16 * z, 16), :] = pieces[k]
+        for k in range(8):
+            turned = []
+            for half in range(2):
+                at = pl.ds(16 * k + 8 * half, 8)
+                c2, s2 = second_cos[at, :], second_sin[at, :]
+                c = c1 * c2 - s1 * s2
+                s = s1 * c2 + c1 * s2
+                re, im = held[0, b1, at, :], held[1, b1, at, :]
+                turned.append((re * c + im * s, im * c - re * s))
+            for z in range(2):
+                low, high = flip(turned[0][z], turned[1][z], maps)
+                ready[b1 * 8 + k, pl.ds(16 * z, 8), :] = low
+                ready[b1 * 8 + k, pl.ds(16 * z + 8, 8), :] = high
         return carry
 
-    lax.fori_loop(0, PRE_BOXES, one, 0)
+    for p in range(PARTS):
+        copies[p].wait()
+        lax.fori_loop(BOXES * p, BOXES * (p + 1), one, 0, unroll=2)
+        sends[p].start()
+    for send in sends:
+        send.wait()
 
 
 def pre(coeffs, deform):
-    smem = pl.BlockSpec(memory_space=pltpu.SMEM)
     return pl.pallas_call(
         pre_kernel,
-        grid=(16 // PRE_BOXES,),
-        out_shape=jax.ShapeDtypeStruct((128, 32, 128), jnp.float32),
+        out_shape=jax.ShapeDtypeStruct((128, 32, LANES), jnp.float32),
         in_specs=[
-            smem,
-            pl.BlockSpec((2, 8, LANES), lambda i: (0, 0, 0)),
-            pl.BlockSpec((2, 1, PRE_BOXES, 1, 128, LANES), lambda i: (0, 0, i, 0, 0, 0)),
+            pl.BlockSpec(memory_space=pltpu.SMEM),
+            pl.BlockSpec(memory_space=pltpu.HBM),
         ],
-        out_specs=pl.BlockSpec((8 * PRE_BOXES, 32, LANES), lambda i: (i, 0, 0)),
+        out_specs=pl.BlockSpec(memory_space=pltpu.HBM),
         scratch_shapes=[
+            pltpu.VMEM((2, 16, 128, LANES), jnp.float32),
+            pltpu.VMEM((128, 32, LANES), jnp.float32),
             pltpu.VMEM((16, LANES), jnp.float32),
             pltpu.VMEM((16, LANES), jnp.float32),
             pltpu.VMEM((128, LANES), jnp.float32),
             pltpu.VMEM((128, LANES), jnp.float32),
+            pltpu.SemaphoreType.DMA((PARTS,)),
+            pltpu.SemaphoreType.DMA((PARTS,)),
         ],
+        compiler_params=pltpu.CompilerParams(vmem_limit_bytes=60 * MIB),
         cost_estimate=pl.CostEstimate(
             flops=10 * MIB, bytes_accessed=4 * MIB, transcendentals=0
         ),
-    )(deform, jnp.asarray(lane_nodes()), coeffs)
+    )(deform, coeffs)
 
 
 def phase_rows(tables, deform, store):
@@ -283,7 +302,7 @@
 
 
 def build_kernel(
-    deform, nodes, inner, outer, wide, px, py, px_last, m1, m2, first, second, rows_in, rows_out
+    deform, inner, outer, wide, px, py, px_last, m1_out, m2_out, first, second, rows_in, rows_out, m1, m2, sems
 ):
     phase_rows(inner, deform, rows_in)
     phase_rows(outer, deform, rows_out)
@@ -309,6 +328,11 @@
         return carry
 
     lax.fori_loop(0, 16, group, 0)
+    copies = [
+        pltpu.make_async_copy(m1, m1_out, sems.at[0]),
+        pltpu.make_async_copy(m2, m2_out, sems.at[1]),
+    ]
+    copies[0].start()
 
     rows = [[rows_out[c, z, 0:1, :] for z in range(2)] for c in range(2)]
     for c5, value in enumerate(chain(rows, 512, 768, 896)):
@@ -321,9 +345,10 @@
                     m2[0, pl.ds(at, 32), :] = high
                     m2[1, pl.ds(at, 32), :] = low
 
+    copies[1].start()
     sx = lax.axis_index("sx").astype(jnp.float32)
     sy = lax.axis_index("sy").astype(jnp.float32)
-    y1, y2 = warp(deform, nodes[0], nodes[1])
+    y1, y2 = warp(deform, *lane_nodes())
     c, s = turn(y1[0:1] * (iota((16, LANES), 0).astype(jnp.float32) + (16.0 * sx + 0.5)))
     scale = math.sqrt(0.5) ** 7
     first[0] = c * scale
@@ -331,27 +356,32 @@
     c, s = turn(y2[0:1] * (iota((128, LANES), 0).astype(jnp.float32) + (128.0 * sy + 0.5)))
     second[0] = c
     second[1] = s
+    for copy in copies:
+        copy.wait()
 
 
 def build(deform):
     inner, outer = column_tables()
-    consts = [lane_nodes(), inner, outer, pattern_y_first(), pattern_x(), pattern_y(), pattern_x_last()]
+    consts = [inner, outer, pattern_y_first(), pattern_x(), pattern_y(), pattern_x_last()]
     vmem = pl.BlockSpec(memory_space=pltpu.VMEM)
     return pl.pallas_call(
         build_kernel,
         out_shape=[
-            jax.ShapeDtypeStruct((16, 512, 256), jnp.bfloat16),
-            jax.ShapeDtypeStruct((2, 512, 512), jnp.bfloat16),
+            pltpu.HBM((16, 512, 256), jnp.bfloat16),
+            pltpu.HBM((2, 512, 512), jnp.bfloat16),
             jax.ShapeDtypeStruct((2, 16, LANES), jnp.float32),
             jax.ShapeDtypeStruct((2, 128, LANES), jnp.float32),
         ],
-        in_specs=[pl.BlockSpec(memory_space=pltpu.SMEM)] + [vmem] * 7,
-        out_specs=[vmem] * 4,
+        in_specs=[pl.BlockSpec(memory_space=pltpu.SMEM)] + [vmem] * 6,
+        out_specs=[pl.BlockSpec(memory_space=pltpu.HBM)] * 2 + [vmem] * 2,
         scratch_shapes=[
             pltpu.VMEM((2, 2, 16, 512), jnp.float32),
             pltpu.VMEM((2, 2, 8, 1024), jnp.float32),
+            pltpu.VMEM((16, 512, 256), jnp.bfloat16),
+            pltpu.VMEM((2, 512, 512), jnp.bfloat16),
+            pltpu.SemaphoreType.DMA((2,)),
         ],
-        compiler_params=pltpu.CompilerParams(vmem_limit_bytes=32 * MIB),
+        compiler_params=pltpu.CompilerParams(vmem_limit_bytes=16 * MIB),
         cost_estimate=pl.CostEstimate(
             flops=6000 * MIB, bytes_accessed=40 * MIB, transcendentals=0
         ),
@@ -362,7 +392,16 @@
     return jnp.dot(a, b, preferred_element_type=jnp.float32)
 
 
-def post_kernel(m1, m2, first, second, got, out, high, low, acc, done, sems):
+def post_kernel(
+    m1_in, m2_in, first, second, got, out, m1, m2, high, low, acc, done, cos, sin, sems, in_sems
+):
+    loads = [
+        pltpu.make_async_copy(m1_in.at[pl.ds(4 * p, 4)], m1.at[pl.ds(4 * p, 4)], in_sems.at[p])
+        for p in range(4)
+    ] + [pltpu.make_async_copy(m2_in, m2, in_sems.at[4])]
+    for load in loads:
+        load.start()
+
     def stage_one(g, carry):
         gx, gy = g // 4, g % 4
         x = jnp.concatenate(
@@ -380,9 +419,12 @@
                 low[c13, at, pl.ds(128 * c2, 128)] = yl[piece]
         return carry
 
-    lax.fori_loop(0, 16, stage_one, 0)
-
-    lane = iota((16, LANES), 1)
+    for p in range(4):
+        loads[p].wait()
+        lax.fori_loop(4 * p, 4 * p + 4, stage_one, 0, unroll=4)
+    loads[4].wait()
+
+    maps = flip_maps()
 
     def copies(c13):
         return [
@@ -401,19 +443,27 @@
             c2, s2 = second[0], second[1]
             c = c1 * c2 - s1 * s2
             s = s1 * c2 + c1 * s2
-            turned = []
-            for z in range(2):
-                pieces = []
-                for cy in range(8):
-                    top, rest = cy >> 2, cy & 3
-                    at = pl.multiple_of(128 * c57, 128) + 32 * rest + 16 * z
-                    pieces.append(acc[pl.ds(at, 16), pl.ds(128 * top, 128)])
-                turned.append(jnp.concatenate(exchange(pieces, lane), axis=0).T)
-            done[0, cx] = turned[0] * c - turned[1] * s
-            done[1, cx] = turned[1] * c + turned[0] * s
+            cos[...] = c
+            sin[...] = s
+            for cy in range(8):
+                at = pl.multiple_of(128 * c57, 128) + 32 * (cy & 3)
+                part = pl.ds(128 * (cy >> 2), 128)
+                re, im = [
+                    flip(
+                        acc[pl.ds(at + 16 * z, 8), part],
+                        acc[pl.ds(at + 16 * z + 8, 8), part],
+                        maps,
+                    )
+                    for z in range(2)
+                ]
+                for half in range(2):
+                    rows = pl.ds(64 * half + cy, 8, stride=8)
+                    c, s = cos[rows, :], sin[rows, :]
+                    done[0, cx, rows, :] = re[half] * c - im[half] * s
+                    done[1, cx, rows, :] = im[half] * c + re[half] * s
             return carry
 
-        lax.fori_loop(0, 4, finish, 0)
+        lax.fori_loop(0, 4, finish, 0, unroll=4)
         for copy in copies(c13):
             copy.start()
     for c13 in range(4):
@@ -426,20 +476,25 @@
     return pl.pallas_call(
         post_kernel,
         out_shape=jax.ShapeDtypeStruct((2, 16, 128, LANES), jnp.float32),
-        in_specs=[vmem] * 5,
-        out_specs=pl.BlockSpec(memory_space=pl.ANY),
+        in_specs=[pl.BlockSpec(memory_space=pltpu.HBM)] * 2 + [vmem] * 3,
+        out_specs=pl.BlockSpec(memory_space=pltpu.HBM),
         scratch_shapes=[
+            pltpu.VMEM((16, 512, 256), jnp.bfloat16),
+            pltpu.VMEM((2, 512, 512), jnp.bfloat16),
             pltpu.VMEM((4, 512, 256), jnp.bfloat16),
             pltpu.VMEM((4, 512, 256), jnp.bfloat16),
             pltpu.VMEM((512, 256), jnp.float32),
             pltpu.VMEM((2, 16, 128, LANES), jnp.float32),
+            pltpu.VMEM((128, LANES), jnp.float32),
+            pltpu.VMEM((128, LANES), jnp.float32),
             pltpu.SemaphoreType.DMA((2, 4)),
+            pltpu.SemaphoreType.DMA((5,)),
         ],
-        compiler_params=pltpu.CompilerParams(vmem_limit_bytes=32 * MIB),
+        compiler_params=pltpu.CompilerParams(vmem_limit_bytes=16 * MIB),
         cost_estimate=pl.CostEstimate(
             flops=4000 * MIB, bytes_accessed=10 * MIB, transcendentals=0
         ),
-    )(m1, m2, first, second, got)
+    )(*[pltpu.with_memory_space_constraint(m, pltpu.HBM) for m in (m1, m2)], first, second, got)
 
 
 def body(coeffs, deform):

time: 66.5 us -> 52.1 us (0.78)
  Pallas kernels: 33.1 us -> 23 us
  local copies, waits for them, and re-layouts: 6.37 us -> 0.05 us
  waiting for transfers between devices: 15.5 us -> 17.6 us
    pallas_call x1, Pallas kernels: 14.1 us -> 6.91 us  [post(): pl.pallas_call(post_kernel, out_shape=jax.ShapeDtypeStruct((2, 16, 128, L...]
    unnamed x24 -> x14, local copies, waits for them, and re-layouts: 6.37 us -> 0.05 us
    pallas_call x2, Pallas kernels: 19 us -> 16.1 us  [the longest x1 12.3 us: build(): pl.pallas_call(build_kernel, out_shape=[pltpu.HBM((16, 512, 256), jnp.bfl...]
    all_to_all x1, waiting for transfers between devices: 15.5 us -> 17.6 us  [body(): got = lax.all_to_all(sent, ('sx', 'sy'), 0, 0, tiled=True)]
  transfers between devices with their start and end apart: 1 -> 1, of which waited for: 1 -> 1; matrix products, arithmetic and copies ran while one was open for 0% -> 0% of each run, Pallas kernels for 17% -> 24%
where the time goes in v2:
time: 52.1 us; the launch traced here: 51.9 us
  Pallas kernels  23 us (44%)
  waiting for transfers between devices  17.6 us (34%)
  starting transfers between devices  11.1 us (21%)
    all_to_all x1, waiting for transfers between devices, body(): got = lax.all_to_all(sent, ('sx', 'sy'), 0, 0, tiled=True)  17.6 us
    pallas_call x1, Pallas kernels, build(): pl.pallas_call(build_kernel, out_shape=[pltpu.HBM((16, 512, 256), jnp.bfl...  12.3 us
    all_to_all x1, starting transfers between devices, body(): got = lax.all_to_all(sent, ('sx', 'sy'), 0, 0, tiled=True)  11.1 us
    pallas_call x1, Pallas kernels, post(): pl.pallas_call(post_kernel, out_shape=jax.ShapeDtypeStruct((2, 16, 128, L...  6.91 us
    pallas_call x1, Pallas kernels, pre(): pl.pallas_call(pre_kernel, out_shape=jax.ShapeDtypeStruct((128, 32, LANES...  3.77 us
  transfers between devices with their start and end apart: 1, of which 1 were waited for; matrix products, arithmetic and copies ran while one was open for 0% of the time, Pallas kernels for 24%

profile of v2, /device:TPU:0, one launch (start us, length us, event | category | flops | bytes accessed | tf_op | source)
XLA Modules:
  0.0 51.9 jit_solution(14039934879704502932)
XLA Ops:
  0.0 3.8 %shard_map.83 = f32[128,32,128]{2,1,0:T(8,128)} custom-call(f32[2,4]{1,0:T(2,128)} %deform.3, f32[2,1,16,1,128,128]{5,4,3,2,1,0:T(8,128)} %coeffs.1), custom_call_target="tpu_custom_call" | custom-call | flops 10485760 | bytes 4194304 | tf_op jit(solution)/shard_map/pallas_call | solution.py:259
  3.8 0.0 copy-start
  3.8 0.0 copy-start.1
  3.8 0.0 copy-start.2
  3.8 0.0 copy-start.3
  3.8 0.0 copy-start.4
  3.8 0.0 copy-start.5
  3.9 0.0 copy-start.6
  3.9 11.1 %all-to-all-start = ((f32[128,32,128]{2,1,0:T(8,128)}), f32[128,32,128]{2,1,0:T(8,128)S(1)}, u32[]{:S(2)}, u32[]{:S(2)}) async-start(f32[128,32,128]{2,1,0:T(8,128)} %shard_map.83), calls=%async_computation | async-start | bytes 4194304 | tf_op jit(solution)/shard_map/all_to_all | solution.py:502
  15.0 0.0 copy-done
  15.0 0.0 copy-done.1
  15.0 0.0 copy-done.2
  15.1 0.0 copy-done.3
  15.1 0.0 copy-done.4
  15.1 0.0 copy-done.5
  15.1 0.0 copy-done.6
  15.1 12.3 %shard_map.82 = (bf16[16,512,256]{2,1,0:T(8,128)(2,1)}, bf16[2,512,512]{2,1,0:T(8,128)(2,1)}, f32[2,16,128]{2,1,0:T(8,128)S(1)}, f32[2,128,128]{2,1,0:T(8,128)S(1)}) custom-call(f32[2,4]{1,0:T(2,128)S(1)} %copy-done, f32[5,16,512]{2,1,0:T(8,128)S(1)} %copy-done.3, f32[5,8,1024]{2,1,0:T(8,128)S(1)} %copy-done.2, f32[256,512]{1,0:T(8,128)S(1)} %copy-done.1, ...), custom_call_target="tpu_custom_call" | custom-call | flops 6291456000 | bytes 41943040 | tf_op jit(solution)/shard_map/pallas_call | solution.py:367
  27.4 17.6 %all-to-all-done.got = f32[128,32,128]{2,1,0:T(8,128)S(1)} async-done(((f32[128,32,128]{2,1,0:T(8,128)}), f32[128,32,128]{2,1,0:T(8,128)S(1)}, u32[]{:S(2)}, u32[]{:S(2)}) %all-to-all-start) | async-done | bytes 2097184 | tf_op jit(solution)/shard_map/all_to_all | solution.py:502
  45.0 6.9 %shard_map.84 = f32[2,16,128,128]{3,2,1,0:T(8,128)} custom-call(bf16[16,512,256]{2,1,0:T(8,128)(2,1)} %get-tuple-element.9.m1_in, bf16[2,512,512]{2,1,0:T(8,128)(2,1)} %get-tuple-element.10.m2_in, f32[2,16,128]{2,1,0:T(8,128)S(1)} %get-tuple-element.11.first, f32[2,128,128]{2,1,0:T(8,128)S(1)} %get-tuple-element.12.second, f32[128,32,128]{2,1,0:T(8,128)S(1)} %all-to-all-done.got), custom_call_target="tpu_custom_call" | custom-call | flops 4194304000 | bytes 10485760 | tf_op jit(solution)/shard_map/pallas_call | solution.py:476
Async XLA Ops:
  3.8 11.2 %copy-start = (f32[2,4]{1,0:T(2,128)S(1)}, f32[2,4]{1,0:T(2,128)}, u32[]{:S(2)}) copy-start(f32[2,4]{1,0:T(2,128)} %deform.3) | copy-start | bytes 100
  3.8 11.2 %copy-start.1 = (f32[256,512]{1,0:T(8,128)S(1)}, f32[256,512]{1,0:T(8,128)}, u32[]{:S(2)}) copy-start(f32[256,512]{1,0:T(8,128)} %constant.14.clone.wide) | copy-start | bytes 1572868
  3.8 11.2 %copy-start.2 = (f32[5,8,1024]{2,1,0:T(8,128)S(1)}, f32[5,8,1024]{2,1,0:T(8,128)}, u32[]{:S(2)}) copy-start(f32[5,8,1024]{2,1,0:T(8,128)} %constant.13.clone.outer) | copy-start | bytes 491524
  3.8 11.2 %copy-start.3 = (f32[5,16,512]{2,1,0:T(8,128)S(1)}, f32[5,16,512]{2,1,0:T(8,128)}, u32[]{:S(2)}) copy-start(f32[5,16,512]{2,1,0:T(8,128)} %constant.12.clone.inner) | copy-start | bytes 491524
  3.8 11.2 %copy-start.4 = (f32[128,256]{1,0:T(8,128)S(1)}, f32[128,256]{1,0:T(8,128)}, u32[]{:S(2)}) copy-start(f32[128,256]{1,0:T(8,128)} %constant.15.clone.px) | copy-start | bytes 393220
  3.8 11.2 %copy-start.5 = (f32[64,128]{1,0:T(8,128)S(1)}, f32[64,128]{1,0:T(8,128)}, u32[]{:S(2)}) copy-start(f32[64,128]{1,0:T(8,128)} %constant.16.clone.py) | copy-start | bytes 98308
  3.9 11.2 %copy-start.6 = (f32[32,64]{1,0:T(8,128)S(1)}, f32[32,64]{1,0:T(8,128)}, u32[]{:S(2)}) copy-start(f32[32,64]{1,0:T(8,128)} %constant.17.clone.px_last) | copy-start | bytes 24580
  3.9 41.1 %all-to-all-start = ((f32[128,32,128]{2,1,0:T(8,128)}), f32[128,32,128]{2,1,0:T(8,128)S(1)}, u32[]{:S(2)}, u32[]{:S(2)}) async-start(f32[128,32,128]{2,1,0:T(8,128)} %shard_map.83), calls=%async_computation | async-start | bytes 4194304 | tf_op jit(solution)/shard_map/all_to_all | solution.py:502

commit v3 on v2

--- a/solution.py
+++ b/solution.py
@@ -6,6 +6,7 @@
 from jax import lax
 from jax.experimental import pallas as pl
 from jax.experimental.pallas import tpu as pltpu
+from jax.sharding import Mesh
 from jax.sharding import PartitionSpec as P
 
 NODES = 4
@@ -197,24 +198,29 @@
     return pick((lane >> 2) & 3), pick(lane & 3)
 
 
+def position():
+    at = lax.axis_index
+    return at("x_hi") * 8 + at("y") * 2 + at("core"), at("z") * 2 + at("x_lo")
+
+
 def iota(shape, dim):
     return lax.broadcasted_iota(jnp.int32, shape, dim)
 
 
-PARTS = 4
-BOXES = 16 // PARTS
+PARTS = 8
+CHUNKS = (2, 4, 4, 2, 64, LANES)
 
 
 def pre_kernel(deform, coeffs, out, held, ready, first_cos, first_sin, second_cos, second_sin, sems, out_sems):
     copies = [
         pltpu.make_async_copy(
-            coeffs.at[:, 0, pl.ds(BOXES * p, BOXES), 0], held.at[:, pl.ds(BOXES * p, BOXES)], sems.at[p]
+            coeffs.at[:, 0, pl.ds(2 * p, 2), 0], held.at[:, pl.ds(2 * p, 2)], sems.at[p]
         )
         for p in range(PARTS)
     ]
     sends = [
         pltpu.make_async_copy(
-            ready.at[pl.ds(8 * BOXES * p, 8 * BOXES)], out.at[pl.ds(8 * BOXES * p, 8 * BOXES)], out_sems.at[p]
+            ready.at[:, :, p & 3, p >> 2], out.at[:, :, p & 3, p >> 2], out_sems.at[p]
         )
         for p in range(PARTS)
     ]
@@ -222,16 +228,15 @@
         copy.start()
 
     nodes = lane_nodes()
-    sx = lax.axis_index("sx").astype(jnp.float32)
-    sy = lax.axis_index("sy").astype(jnp.float32)
+    sx, sy = [v.astype(jnp.float32) for v in position()]
     y1, y2 = warp(deform, (nodes[0] + sx) * (1 / 16), (nodes[1] + sy) * (1 / 8))
     y1, y2 = y1[0:1] * 16.0, y2[0:1] * 8.0
     first_cos[...], first_sin[...] = turn(y1 * (iota((16, LANES), 0).astype(jnp.float32) + 0.5))
     second_cos[...], second_sin[...] = turn(y2 * (iota((128, LANES), 0).astype(jnp.float32) + 0.5))
     maps = flip_maps()
 
-    def one(b1, carry):
-        c1, s1 = first_cos[pl.ds(b1, 1), :], first_sin[pl.ds(b1, 1), :]
+    def one(b1):
+        c1, s1 = first_cos[b1 : b1 + 1, :], first_sin[b1 : b1 + 1, :]
         for k in range(8):
             turned = []
             for half in range(2):
@@ -243,14 +248,18 @@
                 turned.append((re * c + im * s, im * c - re * s))
             for z in range(2):
                 low, high = flip(turned[0][z], turned[1][z], maps)
-                ready[b1 * 8 + k, pl.ds(16 * z, 8), :] = low
-                ready[b1 * 8 + k, pl.ds(16 * z + 8, 8), :] = high
-        return carry
-
-    for p in range(PARTS):
-        copies[p].wait()
-        lax.fori_loop(BOXES * p, BOXES * (p + 1), one, 0, unroll=2)
-        sends[p].start()
+                at = 32 * (k & 1) + 16 * z
+                spot = (b1 & 1, k >> 1, (b1 >> 1) & 3, b1 >> 3)
+                ready[(*spot, pl.ds(at, 8))] = low
+                ready[(*spot, pl.ds(at + 8, 8))] = high
+
+    for q in range(0, PARTS, 2):
+        for p in (q, q + 1):
+            copies[p].wait()
+        for b1 in range(2 * q, 2 * q + 4):
+            one(b1)
+        for p in (q, q + 1):
+            sends[p].start()
     for send in sends:
         send.wait()
 
@@ -258,7 +267,7 @@
 def pre(coeffs, deform):
     return pl.pallas_call(
         pre_kernel,
-        out_shape=jax.ShapeDtypeStruct((128, 32, LANES), jnp.float32),
+        out_shape=jax.ShapeDtypeStruct(CHUNKS, jnp.float32),
         in_specs=[
             pl.BlockSpec(memory_space=pltpu.SMEM),
             pl.BlockSpec(memory_space=pltpu.HBM),
@@ -266,7 +275,7 @@
         out_specs=pl.BlockSpec(memory_space=pltpu.HBM),
         scratch_shapes=[
             pltpu.VMEM((2, 16, 128, LANES), jnp.float32),
-            pltpu.VMEM((128, 32, LANES), jnp.float32),
+            pltpu.VMEM(CHUNKS, jnp.float32),
             pltpu.VMEM((16, LANES), jnp.float32),
             pltpu.VMEM((16, LANES), jnp.float32),
             pltpu.VMEM((128, LANES), jnp.float32),
@@ -307,13 +316,13 @@
     phase_rows(inner, deform, rows_in)
     phase_rows(outer, deform, rows_out)
 
-    def chain(rows, at_x, at_y, at_last):
+    def chain(rows, at_x, at_y, at_last, keep):
         last = jnp.concatenate(
             [level(px_last[...], rows, c, slice(at_last, at_last + 64)) for c in range(2)], axis=0
         )
         parts = [dot(last, level(py[...], rows, c, slice(at_y, at_y + 128))) for c in range(2)]
         joined = jnp.concatenate(
-            [parts[cy][32 * cx : 32 * cx + 32] for cx in range(2) for cy in range(2)], axis=0
+            [parts[cy][32 * cx : 32 * cx + keep] for cx in range(2) for cy in range(2)], axis=0
         )
         return [
             dot(joined, level(px[...], rows, c, slice(at_x, at_x + 256))) for c in range(2)
@@ -321,10 +330,10 @@
 
     def group(g, carry):
         rows = [[rows_in[c, z, pl.ds(g, 1), :] for z in range(2)] for c in range(2)]
-        for c, value in enumerate(chain(rows, 0, 256, 384)):
+        for c, value in enumerate(chain(rows, 0, 256, 384, 16)):
             high, low = split(value)
-            m1[g, pl.ds(128 * c, 128), :] = high
-            m1[g, pl.ds(256 + 128 * c, 128), :] = low
+            m1[g, pl.ds(64 * c, 64), :] = high
+            m1[g, pl.ds(128 + 64 * c, 64), :] = low
         return carry
 
     lax.fori_loop(0, 16, group, 0)
@@ -335,7 +344,7 @@
     copies[0].start()
 
     rows = [[rows_out[c, z, 0:1, :] for z in range(2)] for c in range(2)]
-    for c5, value in enumerate(chain(rows, 512, 768, 896)):
+    for c5, value in enumerate(chain(rows, 512, 768, 896, 32)):
         for c4 in range(2):
             block = dot(value, level(wide[...], rows, c4, slice(0, 512)))
             for c7 in range(2):
@@ -346,8 +355,7 @@
                     m2[1, pl.ds(at, 32), :] = low
 
     copies[1].start()
-    sx = lax.axis_index("sx").astype(jnp.float32)
-    sy = lax.axis_index("sy").astype(jnp.float32)
+    sx, sy = [v.astype(jnp.float32) for v in position()]
     y1, y2 = warp(deform, *lane_nodes())
     c, s = turn(y1[0:1] * (iota((16, LANES), 0).astype(jnp.float32) + (16.0 * sx + 0.5)))
     scale = math.sqrt(0.5) ** 7
@@ -367,7 +375,7 @@
     return pl.pallas_call(
         build_kernel,
         out_shape=[
-            pltpu.HBM((16, 512, 256), jnp.bfloat16),
+            pltpu.HBM((16, 256, 256), jnp.bfloat16),
             pltpu.HBM((2, 512, 512), jnp.bfloat16),
             jax.ShapeDtypeStruct((2, 16, LANES), jnp.float32),
             jax.ShapeDtypeStruct((2, 128, LANES), jnp.float32),
@@ -377,7 +385,7 @@
         scratch_shapes=[
             pltpu.VMEM((2, 2, 16, 512), jnp.float32),
             pltpu.VMEM((2, 2, 8, 1024), jnp.float32),
-            pltpu.VMEM((16, 512, 256), jnp.bfloat16),
+            pltpu.VMEM((16, 256, 256), jnp.bfloat16),
             pltpu.VMEM((2, 512, 512), jnp.bfloat16),
             pltpu.SemaphoreType.DMA((2,)),
         ],
@@ -396,33 +404,38 @@
     m1_in, m2_in, first, second, got, out, m1, m2, high, low, acc, done, cos, sin, sems, in_sems
 ):
     loads = [
-        pltpu.make_async_copy(m1_in.at[pl.ds(4 * p, 4)], m1.at[pl.ds(4 * p, 4)], in_sems.at[p])
-        for p in range(4)
-    ] + [pltpu.make_async_copy(m2_in, m2, in_sems.at[4])]
+        pltpu.make_async_copy(m1_in.at[pl.ds(8 * p, 8)], m1.at[pl.ds(8 * p, 8)], in_sems.at[p])
+        for p in range(2)
+    ] + [pltpu.make_async_copy(m2_in, m2, in_sems.at[2])]
     for load in loads:
         load.start()
 
-    def stage_one(g, carry):
-        gx, gy = g // 4, g % 4
-        x = jnp.concatenate(
-            [got[pl.ds((4 * gx + i) * 8 + 2 * gy, 2)].reshape(64, LANES) for i in range(4)], axis=0
-        )
-        xh, xl = split(x)
-        res = mul(m1[g], jnp.concatenate([xh, xl], axis=1))
-        res = res[:256, :128] + (res[:256, 128:] + res[256:, :128])
-        yh, yl = split(res)
-        for c13 in range(4):
-            for c2 in range(2):
-                piece = slice(64 * c13 + 32 * c2, 64 * c13 + 32 * c2 + 32)
-                at = pl.ds(pl.multiple_of(32 * g, 32), 32)
-                high[c13, at, pl.ds(128 * c2, 128)] = yh[piece]
-                low[c13, at, pl.ds(128 * c2, 128)] = yl[piece]
-        return carry
-
-    for p in range(4):
+    def stage_one(g, matrix):
+        gx, gy = g >> 2, g & 3
+        x = [[], []]
+        for i in range(4):
+            chunk = (i & 1) * 64 + gy * 16 + ((gx & 1) * 2 + (i >> 1)) * 4 + (gx >> 1) * 2
+            for j in range(2):
+                re, im = got[chunk + j, 0:16, :], got[chunk + j, 16:32, :]
+                x[0] += [re, im]
+                x[1] += [im, -re]
+        x = [split(jnp.concatenate(v, axis=0)) for v in x]
+        res = mul(matrix, jnp.concatenate([*x[0], *x[1]], axis=1))
+        for z in range(2):
+            part = res[:, 256 * z : 256 * z + 256]
+            yh, yl = split(part[:128, :128] + (part[:128, 128:] + part[128:, :128]))
+            at = pl.ds(32 * g + 16 * z, 16)
+            for c13 in range(4):
+                for c2 in range(2):
+                    piece = slice(32 * c13 + 16 * c2, 32 * c13 + 16 * c2 + 16)
+                    high[c13, at, pl.ds(128 * c2, 128)] = yh[piece]
+                    low[c13, at, pl.ds(128 * c2, 128)] = yl[piece]
+
+    for p in range(2):
         loads[p].wait()
-        lax.fori_loop(4 * p, 4 * p + 4, stage_one, 0, unroll=4)
-    loads[4].wait()
+        for g in range(8 * p, 8 * p + 8):
+            stage_one(g, m1[g])
+    loads[2].wait()
 
     maps = flip_maps()
 
@@ -479,7 +492,7 @@
         in_specs=[pl.BlockSpec(memory_space=pltpu.HBM)] * 2 + [vmem] * 3,
         out_specs=pl.BlockSpec(memory_space=pltpu.HBM),
         scratch_shapes=[
-            pltpu.VMEM((16, 512, 256), jnp.bfloat16),
+            pltpu.VMEM((16, 256, 256), jnp.bfloat16),
             pltpu.VMEM((2, 512, 512), jnp.bfloat16),
             pltpu.VMEM((4, 512, 256), jnp.bfloat16),
             pltpu.VMEM((4, 512, 256), jnp.bfloat16),
@@ -488,23 +501,34 @@
             pltpu.VMEM((128, LANES), jnp.float32),
             pltpu.VMEM((128, LANES), jnp.float32),
             pltpu.SemaphoreType.DMA((2, 4)),
-            pltpu.SemaphoreType.DMA((5,)),
+            pltpu.SemaphoreType.DMA((3,)),
         ],
         compiler_params=pltpu.CompilerParams(vmem_limit_bytes=16 * MIB),
         cost_estimate=pl.CostEstimate(
             flops=4000 * MIB, bytes_accessed=10 * MIB, transcendentals=0
         ),
-    )(*[pltpu.with_memory_space_constraint(m, pltpu.HBM) for m in (m1, m2)], first, second, got)
+    )(
+        *[pltpu.with_memory_space_constraint(m, pltpu.HBM) for m in (m1, m2)],
+        first,
+        second,
+        got,
+    )
 
 
 def body(coeffs, deform):
     sent = pre(coeffs, deform)
-    got = lax.all_to_all(sent, ("sx", "sy"), 0, 0, tiled=True)
+    sent = sent.reshape(128, 32, LANES)
+    got = lax.all_to_all(sent, ("core", "z", "y", "x_hi", "x_lo"), 0, 0, tiled=True)
     return post(*build(deform), got)
 
 
 def solution(mesh):
-    placed = (P(None, "sx", None, "sy", None, None), P())
+    fine = Mesh(mesh.devices.reshape(2, 4, 2, 4, 2), ("x_hi", "y", "core", "z", "x_lo"))
+    sx, sy = ("x_hi", "y", "core"), ("z", "x_lo")
     return jax.shard_map(
-        body, mesh=mesh, in_specs=placed, out_specs=P(None, "sx", "sy", None), check_vma=False
-    )
+        body,
+        mesh=fine,
+        in_specs=(P(None, sx, None, sy, None, None), P()),
+        out_specs=P(None, sx, sy, None),
+        check_vma=False,
+    )

time: 52.1 us -> 50.6 us (0.971)
  Pallas kernels: 23 us -> 21 us
    pallas_call x2, Pallas kernels: 16.1 us -> 14.5 us  [the longest x1 10.8 us: build(): pl.pallas_call(build_kernel, out_shape=[pltpu.HBM((16, 256, 256), jnp.bfl...]
  transfers between devices with their start and end apart: 1 -> 1, of which waited for: 1 -> 1; matrix products, arithmetic and copies ran while one was open for 0% -> 0% of each run, Pallas kernels for 24% -> 22%
where the time goes in v3:
time: 50.6 us; the launch traced here: 50.1 us
  Pallas kernels  21 us (42%)
  waiting for transfers between devices  17.7 us (35%)
  starting transfers between devices  11.1 us (22%)
    all_to_all x1, waiting for transfers between devices, body(): lax.all_to_all(sent, ('core', 'z', 'y', 'x_hi', 'x_lo'), 0, 0, tiled=True)  17.7 us
    all_to_all x1, starting transfers between devices, body(): lax.all_to_all(sent, ('core', 'z', 'y', 'x_hi', 'x_lo'), 0, 0, tiled=True)  11.1 us
    pallas_call x1, Pallas kernels, build(): pl.pallas_call(build_kernel, out_shape=[pltpu.HBM((16, 256, 256), jnp.bfl...  10.8 us
    pallas_call x1, Pallas kernels, post(): pl.pallas_call(post_kernel, out_shape=jax.ShapeDtypeStruct((2, 16, 128, L...  6.57 us
    pallas_call x1, Pallas kernels, pre(): pl.pallas_call(pre_kernel, out_shape=jax.ShapeDtypeStruct(CHUNKS, jnp.flo...  3.62 us
  transfers between devices with their start and end apart: 1, of which 1 were waited for; matrix products, arithmetic and copies ran while one was open for 0% of the time, Pallas kernels for 22%

profile of v3, /device:TPU:0, one launch (start us, length us, event | category | flops | bytes accessed | tf_op | source)
XLA Modules:
  0.0 50.1 jit_solution(5316034505610773891)
XLA Ops:
  0.0 3.6 %shard_map.83 = f32[2,4,4,2,64,128]{5,4,3,2,1,0:T(8,128)} custom-call(f32[2,4]{1,0:T(2,128)} %deform.3, f32[2,1,16,1,128,128]{5,4,3,2,1,0:T(8,128)} %coeffs.1), custom_call_target="tpu_custom_call" | custom-call | flops 10485760 | bytes 4194304 | tf_op jit(solution)/shard_map/pallas_call | solution.py:268
  3.6 0.0 copy-start
  3.6 0.0 copy-start.1
  3.7 0.0 copy-start.2
  3.7 0.0 copy-start.3
  3.7 0.0 copy-start.4
  3.7 0.0 copy-start.5
  3.7 0.0 copy-start.6
  3.7 11.1 %all-to-all-start = ((f32[128,32,128]{2,1,0:T(8,128)}), f32[128,32,128]{2,1,0:T(8,128)S(1)}, u32[]{:S(2)}, u32[]{:S(2)}) async-start(f32[128,32,128]{2,1,0:T(8,128)} %bitcast.1), calls=%async_computation | async-start | bytes 4194304 | tf_op jit(solution)/shard_map/all_to_all | solution.py:521
  14.9 0.0 copy-done
  14.9 0.0 copy-done.1
  14.9 0.0 copy-done.2
  14.9 0.0 copy-done.3
  14.9 0.0 copy-done.4
  14.9 0.0 copy-done.5
  14.9 0.0 copy-done.6
  14.9 10.8 %shard_map.82 = (bf16[16,256,256]{2,1,0:T(8,128)(2,1)}, bf16[2,512,512]{2,1,0:T(8,128)(2,1)}, f32[2,16,128]{2,1,0:T(8,128)S(1)}, f32[2,128,128]{2,1,0:T(8,128)S(1)}) custom-call(f32[2,4]{1,0:T(2,128)S(1)} %copy-done, f32[5,16,512]{2,1,0:T(8,128)S(1)} %copy-done.3, f32[5,8,1024]{2,1,0:T(8,128)S(1)} %copy-done.2, f32[256,512]{1,0:T(8,128)S(1)} %copy-done.1, ...), custom_call_target="tpu_custom_call" | custom-call | flops 6291456000 | bytes 41943040 | tf_op jit(solution)/shard_map/pallas_call | solution.py:375
  25.8 17.7 %all-to-all-done.got = f32[128,32,128]{2,1,0:T(8,128)S(1)} async-done(((f32[128,32,128]{2,1,0:T(8,128)}), f32[128,32,128]{2,1,0:T(8,128)S(1)}, u32[]{:S(2)}, u32[]{:S(2)}) %all-to-all-start) | async-done | bytes 2097184 | tf_op jit(solution)/shard_map/all_to_all | solution.py:521
  43.5 6.6 %shard_map.84 = f32[2,16,128,128]{3,2,1,0:T(8,128)} custom-call(bf16[16,256,256]{2,1,0:T(8,128)(2,1)} %get-tuple-element.9.m1_in, bf16[2,512,512]{2,1,0:T(8,128)(2,1)} %get-tuple-element.10.m2_in, f32[2,16,128]{2,1,0:T(8,128)S(1)} %get-tuple-element.11.first, f32[2,128,128]{2,1,0:T(8,128)S(1)} %get-tuple-element.12.second, f32[128,32,128]{2,1,0:T(8,128)S(1)} %all-to-all-done.got), custom_call_target="tpu_custom_call" | custom-call | flops 4194304000 | bytes 10485760 | tf_op jit(solution)/shard_map/pallas_call | solution.py:489
Async XLA Ops:
  3.6 11.2 %copy-start = (f32[2,4]{1,0:T(2,128)S(1)}, f32[2,4]{1,0:T(2,128)}, u32[]{:S(2)}) copy-start(f32[2,4]{1,0:T(2,128)} %deform.3) | copy-start | bytes 100
  3.6 11.2 %copy-start.1 = (f32[256,512]{1,0:T(8,128)S(1)}, f32[256,512]{1,0:T(8,128)}, u32[]{:S(2)}) copy-start(f32[256,512]{1,0:T(8,128)} %constant.14.clone.wide) | copy-start | bytes 1572868
  3.7 11.2 %copy-start.2 = (f32[5,8,1024]{2,1,0:T(8,128)S(1)}, f32[5,8,1024]{2,1,0:T(8,128)}, u32[]{:S(2)}) copy-start(f32[5,8,1024]{2,1,0:T(8,128)} %constant.13.clone.outer) | copy-start | bytes 491524
  3.7 11.2 %copy-start.3 = (f32[5,16,512]{2,1,0:T(8,128)S(1)}, f32[5,16,512]{2,1,0:T(8,128)}, u32[]{:S(2)}) copy-start(f32[5,16,512]{2,1,0:T(8,128)} %constant.12.clone.inner) | copy-start | bytes 491524
  3.7 11.2 %copy-start.4 = (f32[128,256]{1,0:T(8,128)S(1)}, f32[128,256]{1,0:T(8,128)}, u32[]{:S(2)}) copy-start(f32[128,256]{1,0:T(8,128)} %constant.15.clone.px) | copy-start | bytes 393220
  3.7 11.2 %copy-start.5 = (f32[64,128]{1,0:T(8,128)S(1)}, f32[64,128]{1,0:T(8,128)}, u32[]{:S(2)}) copy-start(f32[64,128]{1,0:T(8,128)} %constant.16.clone.py) | copy-start | bytes 98308
  3.7 11.2 %copy-start.6 = (f32[32,64]{1,0:T(8,128)S(1)}, f32[32,64]{1,0:T(8,128)}, u32[]{:S(2)}) copy-start(f32[32,64]{1,0:T(8,128)} %constant.17.clone.px_last) | copy-start | bytes 24580
  3.7 39.8 %all-to-all-start = ((f32[128,32,128]{2,1,0:T(8,128)}), f32[128,32,128]{2,1,0:T(8,128)S(1)}, u32[]{:S(2)}, u32[]{:S(2)}) async-start(f32[128,32,128]{2,1,0:T(8,128)} %bitcast.1), calls=%async_computation | async-start | bytes 4194304 | tf_op jit(solution)/shard_map/all_to_all | solution.py:521

commit v4 on v3

--- a/solution.py
+++ b/solution.py
@@ -401,7 +401,7 @@
 
 
 def post_kernel(
-    m1_in, m2_in, first, second, got, out, m1, m2, high, low, acc, done, cos, sin, sems, in_sems
+    m1_in, m2_in, first, second, got, out, m1, m2, x_high, x_low, high, low, acc, done, cos, sin, sems, in_sems
 ):
     loads = [
         pltpu.make_async_copy(m1_in.at[pl.ds(8 * p, 8)], m1.at[pl.ds(8 * p, 8)], in_sems.at[p])
@@ -410,7 +410,7 @@
     for load in loads:
         load.start()
 
-    def stage_one(g, matrix):
+    def prepare(g):
         gx, gy = g >> 2, g & 3
         x = [[], []]
         for i in range(4):
@@ -419,22 +419,27 @@
                 re, im = got[chunk + j, 0:16, :], got[chunk + j, 16:32, :]
                 x[0] += [re, im]
                 x[1] += [im, -re]
-        x = [split(jnp.concatenate(v, axis=0)) for v in x]
-        res = mul(matrix, jnp.concatenate([*x[0], *x[1]], axis=1))
+        x = jnp.concatenate([jnp.concatenate(v, axis=0) for v in x], axis=1)
+        x_high[g], x_low[g] = split(x)
+
+    def stage_one(g):
+        both = mul(m1[g], x_high[g])
+        yh, yl = split(both[:128] + (mul(m1[g, 0:128], x_low[g]) + both[128:]))
         for z in range(2):
-            part = res[:, 256 * z : 256 * z + 256]
-            yh, yl = split(part[:128, :128] + (part[:128, 128:] + part[128:, :128]))
             at = pl.ds(32 * g + 16 * z, 16)
             for c13 in range(4):
                 for c2 in range(2):
-                    piece = slice(32 * c13 + 16 * c2, 32 * c13 + 16 * c2 + 16)
-                    high[c13, at, pl.ds(128 * c2, 128)] = yh[piece]
-                    low[c13, at, pl.ds(128 * c2, 128)] = yl[piece]
-
+                    rows = slice(32 * c13 + 16 * c2, 32 * c13 + 16 * c2 + 16)
+                    lanes = slice(128 * z, 128 * z + 128)
+                    high[c13, at, pl.ds(128 * c2, 128)] = yh[rows, lanes]
+                    low[c13, at, pl.ds(128 * c2, 128)] = yl[rows, lanes]
+
+    for g in range(16):
+        prepare(g)
     for p in range(2):
         loads[p].wait()
         for g in range(8 * p, 8 * p + 8):
-            stage_one(g, m1[g])
+            stage_one(g)
     loads[2].wait()
 
     maps = flip_maps()
@@ -494,6 +499,8 @@
         scratch_shapes=[
             pltpu.VMEM((16, 256, 256), jnp.bfloat16),
             pltpu.VMEM((2, 512, 512), jnp.bfloat16),
+            pltpu.VMEM((16, 256, 256), jnp.bfloat16),
+            pltpu.VMEM((16, 256, 256), jnp.bfloat16),
             pltpu.VMEM((4, 512, 256), jnp.bfloat16),
             pltpu.VMEM((4, 512, 256), jnp.bfloat16),
             pltpu.VMEM((512, 256), jnp.float32),

time: 50.6 us -> 50.3 us (level)
  no operation moved by 1% of the time
where the time goes in v4:
time: 50.3 us; the launch traced here: 49.8 us
  Pallas kernels  20.8 us (41%)
  waiting for transfers between devices  17.7 us (35%)
  starting transfers between devices  11.1 us (22%)
    all_to_all x1, waiting for transfers between devices, body(): lax.all_to_all(sent, ('core', 'z', 'y', 'x_hi', 'x_lo'), 0, 0, tiled=True)  17.7 us
    all_to_all x1, starting transfers between devices, body(): lax.all_to_all(sent, ('core', 'z', 'y', 'x_hi', 'x_lo'), 0, 0, tiled=True)  11.1 us
    pallas_call x1, Pallas kernels, build(): pl.pallas_call(build_kernel, out_shape=[pltpu.HBM((16, 256, 256), jnp.bfl...  10.8 us
    pallas_call x1, Pallas kernels, post(): pl.pallas_call(post_kernel, out_shape=jax.ShapeDtypeStruct((2, 16, 128, L...  6.31 us
    pallas_call x1, Pallas kernels, pre(): pl.pallas_call(pre_kernel, out_shape=jax.ShapeDtypeStruct(CHUNKS, jnp.flo...  3.62 us
  transfers between devices with their start and end apart: 1, of which 1 were waited for; matrix products, arithmetic and copies ran while one was open for 0% of the time, Pallas kernels for 22%

profile of v4, /device:TPU:0, one launch (start us, length us, event | category | flops | bytes accessed | tf_op | source)
XLA Modules:
  0.0 49.8 jit_solution(15058553218569100371)
XLA Ops:
  0.0 3.6 %shard_map.83 = f32[2,4,4,2,64,128]{5,4,3,2,1,0:T(8,128)} custom-call(f32[2,4]{1,0:T(2,128)} %deform.3, f32[2,1,16,1,128,128]{5,4,3,2,1,0:T(8,128)} %coeffs.1), custom_call_target="tpu_custom_call" | custom-call | flops 10485760 | bytes 4194304 | tf_op jit(solution)/shard_map/pallas_call | solution.py:268
  3.6 0.0 copy-start
  3.6 0.0 copy-start.1
  3.7 0.0 copy-start.2
  3.7 0.0 copy-start.3
  3.7 0.0 copy-start.4
  3.7 0.0 copy-start.5
  3.7 0.0 copy-start.6
  3.7 11.1 %all-to-all-start = ((f32[128,32,128]{2,1,0:T(8,128)}), f32[128,32,128]{2,1,0:T(8,128)S(1)}, u32[]{:S(2)}, u32[]{:S(2)}) async-start(f32[128,32,128]{2,1,0:T(8,128)} %bitcast.1), calls=%async_computation | async-start | bytes 4194304 | tf_op jit(solution)/shard_map/all_to_all | solution.py:528
  14.9 0.0 copy-done
  14.9 0.0 copy-done.1
  14.9 0.0 copy-done.2
  14.9 0.0 copy-done.3
  14.9 0.0 copy-done.4
  14.9 0.0 copy-done.5
  14.9 0.0 copy-done.6
  14.9 10.8 %shard_map.82 = (bf16[16,256,256]{2,1,0:T(8,128)(2,1)}, bf16[2,512,512]{2,1,0:T(8,128)(2,1)}, f32[2,16,128]{2,1,0:T(8,128)S(1)}, f32[2,128,128]{2,1,0:T(8,128)S(1)}) custom-call(f32[2,4]{1,0:T(2,128)S(1)} %copy-done, f32[5,16,512]{2,1,0:T(8,128)S(1)} %copy-done.3, f32[5,8,1024]{2,1,0:T(8,128)S(1)} %copy-done.2, f32[256,512]{1,0:T(8,128)S(1)} %copy-done.1, ...), custom_call_target="tpu_custom_call" | custom-call | flops 6291456000 | bytes 41943040 | tf_op jit(solution)/shard_map/pallas_call | solution.py:375
  25.8 17.7 %all-to-all-done.got = f32[128,32,128]{2,1,0:T(8,128)S(1)} async-done(((f32[128,32,128]{2,1,0:T(8,128)}), f32[128,32,128]{2,1,0:T(8,128)S(1)}, u32[]{:S(2)}, u32[]{:S(2)}) %all-to-all-start) | async-done | bytes 2097184 | tf_op jit(solution)/shard_map/all_to_all | solution.py:528
  43.5 6.3 %shard_map.84 = f32[2,16,128,128]{3,2,1,0:T(8,128)} custom-call(bf16[16,256,256]{2,1,0:T(8,128)(2,1)} %get-tuple-element.9.m1_in, bf16[2,512,512]{2,1,0:T(8,128)(2,1)} %get-tuple-element.10.m2_in, f32[2,16,128]{2,1,0:T(8,128)S(1)} %get-tuple-element.11.first, f32[2,128,128]{2,1,0:T(8,128)S(1)} %get-tuple-element.12.second, f32[128,32,128]{2,1,0:T(8,128)S(1)} %all-to-all-done.got), custom_call_target="tpu_custom_call" | custom-call | flops 4194304000 | bytes 10485760 | tf_op jit(solution)/shard_map/pallas_call | solution.py:494
Async XLA Ops:
  3.6 11.2 %copy-start = (f32[2,4]{1,0:T(2,128)S(1)}, f32[2,4]{1,0:T(2,128)}, u32[]{:S(2)}) copy-start(f32[2,4]{1,0:T(2,128)} %deform.3) | copy-start | bytes 100
  3.6 11.2 %copy-start.1 = (f32[256,512]{1,0:T(8,128)S(1)}, f32[256,512]{1,0:T(8,128)}, u32[]{:S(2)}) copy-start(f32[256,512]{1,0:T(8,128)} %constant.14.clone.wide) | copy-start | bytes 1572868
  3.7 11.2 %copy-start.2 = (f32[5,8,1024]{2,1,0:T(8,128)S(1)}, f32[5,8,1024]{2,1,0:T(8,128)}, u32[]{:S(2)}) copy-start(f32[5,8,1024]{2,1,0:T(8,128)} %constant.13.clone.outer) | copy-start | bytes 491524
  3.7 11.2 %copy-start.3 = (f32[5,16,512]{2,1,0:T(8,128)S(1)}, f32[5,16,512]{2,1,0:T(8,128)}, u32[]{:S(2)}) copy-start(f32[5,16,512]{2,1,0:T(8,128)} %constant.12.clone.inner) | copy-start | bytes 491524
  3.7 11.2 %copy-start.4 = (f32[128,256]{1,0:T(8,128)S(1)}, f32[128,256]{1,0:T(8,128)}, u32[]{:S(2)}) copy-start(f32[128,256]{1,0:T(8,128)} %constant.15.clone.px) | copy-start | bytes 393220
  3.7 11.2 %copy-start.5 = (f32[64,128]{1,0:T(8,128)S(1)}, f32[64,128]{1,0:T(8,128)}, u32[]{:S(2)}) copy-start(f32[64,128]{1,0:T(8,128)} %constant.16.clone.py) | copy-start | bytes 98308
  3.7 11.2 %copy-start.6 = (f32[32,64]{1,0:T(8,128)S(1)}, f32[32,64]{1,0:T(8,128)}, u32[]{:S(2)}) copy-start(f32[32,64]{1,0:T(8,128)} %constant.17.clone.px_last) | copy-start | bytes 24580
  3.7 39.8 %all-to-all-start = ((f32[128,32,128]{2,1,0:T(8,128)}), f32[128,32,128]{2,1,0:T(8,128)S(1)}, u32[]{:S(2)}, u32[]{:S(2)}) async-start(f32[128,32,128]{2,1,0:T(8,128)} %bitcast.1), calls=%async_computation | async-start | bytes 4194304 | tf_op jit(solution)/shard_map/all_to_all | solution.py:528

commit v5 on v4

--- a/solution.py
+++ b/solution.py
@@ -400,12 +400,15 @@
     return jnp.dot(a, b, preferred_element_type=jnp.float32)
 
 
+LOADS = ((0, 4), (4, 16))
+
+
 def post_kernel(
-    m1_in, m2_in, first, second, got, out, m1, m2, x_high, x_low, high, low, acc, done, cos, sin, sems, in_sems
+    m1_in, m2_in, first, second, got, out, m1, m2, x_high, x_low, high, low, acc, done, sems, in_sems
 ):
     loads = [
-        pltpu.make_async_copy(m1_in.at[pl.ds(8 * p, 8)], m1.at[pl.ds(8 * p, 8)], in_sems.at[p])
-        for p in range(2)
+        pltpu.make_async_copy(m1_in.at[pl.ds(a, b - a)], m1.at[pl.ds(a, b - a)], in_sems.at[p])
+        for p, (a, b) in enumerate(LOADS)
     ] + [pltpu.make_async_copy(m2_in, m2, in_sems.at[2])]
     for load in loads:
         load.start()
@@ -436,9 +439,9 @@
 
     for g in range(16):
         prepare(g)
-    for p in range(2):
+    for p, (a, b) in enumerate(LOADS):
         loads[p].wait()
-        for g in range(8 * p, 8 * p + 8):
+        for g in range(a, b):
             stage_one(g)
     loads[2].wait()
 
@@ -458,11 +461,6 @@
         def finish(c57, carry):
             cx = 4 * c13 + c57
             c1, s1 = first[0, pl.ds(cx, 1), :], first[1, pl.ds(cx, 1), :]
-            c2, s2 = second[0], second[1]
-            c = c1 * c2 - s1 * s2
-            s = s1 * c2 + c1 * s2
-            cos[...] = c
-            sin[...] = s
             for cy in range(8):
                 at = pl.multiple_of(128 * c57, 128) + 32 * (cy & 3)
                 part = pl.ds(128 * (cy >> 2), 128)
@@ -476,7 +474,8 @@
                 ]
                 for half in range(2):
                     rows = pl.ds(64 * half + cy, 8, stride=8)
-                    c, s = cos[rows, :], sin[rows, :]
+                    c2, s2 = second[0, rows, :], second[1, rows, :]
+                    c, s = c1 * c2 - s1 * s2, s1 * c2 + c1 * s2
                     done[0, cx, rows, :] = re[half] * c - im[half] * s
                     done[1, cx, rows, :] = im[half] * c + re[half] * s
             return carry
@@ -505,8 +504,6 @@
             pltpu.VMEM((4, 512, 256), jnp.bfloat16),
             pltpu.VMEM((512, 256), jnp.float32),
             pltpu.VMEM((2, 16, 128, LANES), jnp.float32),
-            pltpu.VMEM((128, LANES), jnp.float32),
-            pltpu.VMEM((128, LANES), jnp.float32),
             pltpu.SemaphoreType.DMA((2, 4)),
             pltpu.SemaphoreType.DMA((3,)),
         ],

time: 50.3 us -> 49.8 us (0.990)
  Pallas kernels: 20.8 us -> 20.2 us
    pallas_call x1, Pallas kernels: 6.31 us -> 5.76 us  [post(): pl.pallas_call(post_kernel, out_shape=jax.ShapeDtypeStruct((2, 16, 128, L...]
where the time goes in v5:
time: 49.8 us; the launch traced here: 49.3 us
  Pallas kernels  20.2 us (41%)
  waiting for transfers between devices  17.7 us (36%)
  starting transfers between devices  11.1 us (22%)
    all_to_all x1, waiting for transfers between devices, body(): lax.all_to_all(sent, ('core', 'z', 'y', 'x_hi', 'x_lo'), 0, 0, tiled=True)  17.7 us
    all_to_all x1, starting transfers between devices, body(): lax.all_to_all(sent, ('core', 'z', 'y', 'x_hi', 'x_lo'), 0, 0, tiled=True)  11.1 us
    pallas_call x1, Pallas kernels, build(): pl.pallas_call(build_kernel, out_shape=[pltpu.HBM((16, 256, 256), jnp.bfl...  10.8 us
    pallas_call x1, Pallas kernels, post(): pl.pallas_call(post_kernel, out_shape=jax.ShapeDtypeStruct((2, 16, 128, L...  5.76 us
    pallas_call x1, Pallas kernels, pre(): pl.pallas_call(pre_kernel, out_shape=jax.ShapeDtypeStruct(CHUNKS, jnp.flo...  3.62 us
  transfers between devices with their start and end apart: 1, of which 1 were waited for; matrix products, arithmetic and copies ran while one was open for 0% of the time, Pallas kernels for 22%

profile of v5, /device:TPU:0, one launch (start us, length us, event | category | flops | bytes accessed | tf_op | source)
XLA Modules:
  0.0 49.3 jit_solution(12287790463267629150)
XLA Ops:
  0.0 3.6 %shard_map.83 = f32[2,4,4,2,64,128]{5,4,3,2,1,0:T(8,128)} custom-call(f32[2,4]{1,0:T(2,128)} %deform.3, f32[2,1,16,1,128,128]{5,4,3,2,1,0:T(8,128)} %coeffs.1), custom_call_target="tpu_custom_call" | custom-call | flops 10485760 | bytes 4194304 | tf_op jit(solution)/shard_map/pallas_call | solution.py:268
  3.6 0.0 copy-start
  3.6 0.0 copy-start.1
  3.7 0.0 copy-start.2
  3.7 0.0 copy-start.3
  3.7 0.0 copy-start.4
  3.7 0.0 copy-start.5
  3.7 0.0 copy-start.6
  3.7 11.1 %all-to-all-start = ((f32[128,32,128]{2,1,0:T(8,128)}), f32[128,32,128]{2,1,0:T(8,128)S(1)}, u32[]{:S(2)}, u32[]{:S(2)}) async-start(f32[128,32,128]{2,1,0:T(8,128)} %bitcast.1), calls=%async_computation | async-start | bytes 4194304 | tf_op jit(solution)/shard_map/all_to_all | solution.py:525
  14.9 0.0 copy-done
  14.9 0.0 copy-done.1
  14.9 0.0 copy-done.2
  14.9 0.0 copy-done.3
  14.9 0.0 copy-done.4
  14.9 0.0 copy-done.5
  14.9 0.0 copy-done.6
  14.9 10.8 %shard_map.82 = (bf16[16,256,256]{2,1,0:T(8,128)(2,1)}, bf16[2,512,512]{2,1,0:T(8,128)(2,1)}, f32[2,16,128]{2,1,0:T(8,128)S(1)}, f32[2,128,128]{2,1,0:T(8,128)S(1)}) custom-call(f32[2,4]{1,0:T(2,128)S(1)} %copy-done, f32[5,16,512]{2,1,0:T(8,128)S(1)} %copy-done.3, f32[5,8,1024]{2,1,0:T(8,128)S(1)} %copy-done.2, f32[256,512]{1,0:T(8,128)S(1)} %copy-done.1, ...), custom_call_target="tpu_custom_call" | custom-call | flops 6291456000 | bytes 41943040 | tf_op jit(solution)/shard_map/pallas_call | solution.py:375
  25.8 17.7 %all-to-all-done.got = f32[128,32,128]{2,1,0:T(8,128)S(1)} async-done(((f32[128,32,128]{2,1,0:T(8,128)}), f32[128,32,128]{2,1,0:T(8,128)S(1)}, u32[]{:S(2)}, u32[]{:S(2)}) %all-to-all-start) | async-done | bytes 2097184 | tf_op jit(solution)/shard_map/all_to_all | solution.py:525
  43.5 5.8 %shard_map.84 = f32[2,16,128,128]{3,2,1,0:T(8,128)} custom-call(bf16[16,256,256]{2,1,0:T(8,128)(2,1)} %get-tuple-element.9.m1_in, bf16[2,512,512]{2,1,0:T(8,128)(2,1)} %get-tuple-element.10.m2_in, f32[2,16,128]{2,1,0:T(8,128)S(1)} %get-tuple-element.11.first, f32[2,128,128]{2,1,0:T(8,128)S(1)} %get-tuple-element.12.second, f32[128,32,128]{2,1,0:T(8,128)S(1)} %all-to-all-done.got), custom_call_target="tpu_custom_call" | custom-call | flops 4194304000 | bytes 10485760 | tf_op jit(solution)/shard_map/pallas_call | solution.py:493
Async XLA Ops:
  3.6 11.2 %copy-start = (f32[2,4]{1,0:T(2,128)S(1)}, f32[2,4]{1,0:T(2,128)}, u32[]{:S(2)}) copy-start(f32[2,4]{1,0:T(2,128)} %deform.3) | copy-start | bytes 100
  3.6 11.2 %copy-start.1 = (f32[256,512]{1,0:T(8,128)S(1)}, f32[256,512]{1,0:T(8,128)}, u32[]{:S(2)}) copy-start(f32[256,512]{1,0:T(8,128)} %constant.14.clone.wide) | copy-start | bytes 1572868
  3.7 11.2 %copy-start.2 = (f32[5,8,1024]{2,1,0:T(8,128)S(1)}, f32[5,8,1024]{2,1,0:T(8,128)}, u32[]{:S(2)}) copy-start(f32[5,8,1024]{2,1,0:T(8,128)} %constant.13.clone.outer) | copy-start | bytes 491524
  3.7 11.2 %copy-start.3 = (f32[5,16,512]{2,1,0:T(8,128)S(1)}, f32[5,16,512]{2,1,0:T(8,128)}, u32[]{:S(2)}) copy-start(f32[5,16,512]{2,1,0:T(8,128)} %constant.12.clone.inner) | copy-start | bytes 491524
  3.7 11.2 %copy-start.4 = (f32[128,256]{1,0:T(8,128)S(1)}, f32[128,256]{1,0:T(8,128)}, u32[]{:S(2)}) copy-start(f32[128,256]{1,0:T(8,128)} %constant.15.clone.px) | copy-start | bytes 393220
  3.7 11.2 %copy-start.5 = (f32[64,128]{1,0:T(8,128)S(1)}, f32[64,128]{1,0:T(8,128)}, u32[]{:S(2)}) copy-start(f32[64,128]{1,0:T(8,128)} %constant.16.clone.py) | copy-start | bytes 98308
  3.7 11.2 %copy-start.6 = (f32[32,64]{1,0:T(8,128)S(1)}, f32[32,64]{1,0:T(8,128)}, u32[]{:S(2)}) copy-start(f32[32,64]{1,0:T(8,128)} %constant.17.clone.px_last) | copy-start | bytes 24580
  3.7 39.8 %all-to-all-start = ((f32[128,32,128]{2,1,0:T(8,128)}), f32[128,32,128]{2,1,0:T(8,128)S(1)}, u32[]{:S(2)}, u32[]{:S(2)}) async-start(f32[128,32,128]{2,1,0:T(8,128)} %bitcast.1), calls=%async_computation | async-start | bytes 4194304 | tf_op jit(solution)/shard_map/all_to_all | solution.py:525

commit v6 on v5

--- a/solution.py
+++ b/solution.py
@@ -456,13 +456,16 @@
         ]
 
     for c13 in range(4):
-        acc[...] = mul(m2[0], high[c13]) + (mul(m2[0], low[c13]) + mul(m2[1], high[c13]))
-
-        def finish(c57, carry):
+
+        def finish(c57):
             cx = 4 * c13 + c57
-            c1, s1 = first[0, pl.ds(cx, 1), :], first[1, pl.ds(cx, 1), :]
+            block = pl.ds(128 * c57, 128)
+            acc[block, :] = mul(m2[0, block, :], high[c13]) + (
+                mul(m2[0, block, :], low[c13]) + mul(m2[1, block, :], high[c13])
+            )
+            c1, s1 = first[0, cx : cx + 1, :], first[1, cx : cx + 1, :]
             for cy in range(8):
-                at = pl.multiple_of(128 * c57, 128) + 32 * (cy & 3)
+                at = 128 * c57 + 32 * (cy & 3)
                 part = pl.ds(128 * (cy >> 2), 128)
                 re, im = [
                     flip(
@@ -478,9 +481,9 @@
                     c, s = c1 * c2 - s1 * s2, s1 * c2 + c1 * s2
                     done[0, cx, rows, :] = re[half] * c - im[half] * s
                     done[1, cx, rows, :] = im[half] * c + re[half] * s
-            return carry
-
-        lax.fori_loop(0, 4, finish, 0, unroll=4)
+
+        for c57 in range(4):
+            finish(c57)
         for copy in copies(c13):
             copy.start()
     for c13 in range(4):

time: 49.8 us -> 49.5 us (level)
  no operation moved by 1% of the time
where the time goes in v6:
time: 49.5 us; the launch traced here: 49 us
  Pallas kernels  19.9 us (40%)
  waiting for transfers between devices  17.7 us (36%)
  starting transfers between devices  11.1 us (22%)
    all_to_all x1, waiting for transfers between devices, body(): lax.all_to_all(sent, ('core', 'z', 'y', 'x_hi', 'x_lo'), 0, 0, tiled=True)  17.7 us
    all_to_all x1, starting transfers between devices, body(): lax.all_to_all(sent, ('core', 'z', 'y', 'x_hi', 'x_lo'), 0, 0, tiled=True)  11.1 us
    pallas_call x1, Pallas kernels, build(): pl.pallas_call(build_kernel, out_shape=[pltpu.HBM((16, 256, 256), jnp.bfl...  10.8 us
    pallas_call x1, Pallas kernels, post(): pl.pallas_call(post_kernel, out_shape=jax.ShapeDtypeStruct((2, 16, 128, L...  5.46 us
    pallas_call x1, Pallas kernels, pre(): pl.pallas_call(pre_kernel, out_shape=jax.ShapeDtypeStruct(CHUNKS, jnp.flo...  3.62 us
  transfers between devices with their start and end apart: 1, of which 1 were waited for; matrix products, arithmetic and copies ran while one was open for 0% of the time, Pallas kernels for 22%

profile of v6, /device:TPU:0, one launch (start us, length us, event | category | flops | bytes accessed | tf_op | source)
XLA Modules:
  0.0 49.0 jit_solution(9177012593530193371)
XLA Ops:
  0.0 3.6 %shard_map.83 = f32[2,4,4,2,64,128]{5,4,3,2,1,0:T(8,128)} custom-call(f32[2,4]{1,0:T(2,128)} %deform.3, f32[2,1,16,1,128,128]{5,4,3,2,1,0:T(8,128)} %coeffs.1), custom_call_target="tpu_custom_call" | custom-call | flops 10485760 | bytes 4194304 | tf_op jit(solution)/shard_map/pallas_call | solution.py:268
  3.6 0.0 copy-start
  3.6 0.0 copy-start.1
  3.7 0.0 copy-start.2
  3.7 0.0 copy-start.3
  3.7 0.0 copy-start.4
  3.7 0.0 copy-start.5
  3.7 0.0 copy-start.6
  3.7 11.1 %all-to-all-start = ((f32[128,32,128]{2,1,0:T(8,128)}), f32[128,32,128]{2,1,0:T(8,128)S(1)}, u32[]{:S(2)}, u32[]{:S(2)}) async-start(f32[128,32,128]{2,1,0:T(8,128)} %bitcast.1), calls=%async_computation | async-start | bytes 4194304 | tf_op jit(solution)/shard_map/all_to_all | solution.py:528
  14.9 0.0 copy-done
  14.9 0.0 copy-done.1
  14.9 0.0 copy-done.2
  14.9 0.0 copy-done.3
  14.9 0.0 copy-done.4
  14.9 0.0 copy-done.5
  14.9 0.0 copy-done.6
  14.9 10.8 %shard_map.82 = (bf16[16,256,256]{2,1,0:T(8,128)(2,1)}, bf16[2,512,512]{2,1,0:T(8,128)(2,1)}, f32[2,16,128]{2,1,0:T(8,128)S(1)}, f32[2,128,128]{2,1,0:T(8,128)S(1)}) custom-call(f32[2,4]{1,0:T(2,128)S(1)} %copy-done, f32[5,16,512]{2,1,0:T(8,128)S(1)} %copy-done.3, f32[5,8,1024]{2,1,0:T(8,128)S(1)} %copy-done.2, f32[256,512]{1,0:T(8,128)S(1)} %copy-done.1, ...), custom_call_target="tpu_custom_call" | custom-call | flops 6291456000 | bytes 41943040 | tf_op jit(solution)/shard_map/pallas_call | solution.py:375
  25.8 17.7 %all-to-all-done.got = f32[128,32,128]{2,1,0:T(8,128)S(1)} async-done(((f32[128,32,128]{2,1,0:T(8,128)}), f32[128,32,128]{2,1,0:T(8,128)S(1)}, u32[]{:S(2)}, u32[]{:S(2)}) %all-to-all-start) | async-done | bytes 2097184 | tf_op jit(solution)/shard_map/all_to_all | solution.py:528
  43.5 5.5 %shard_map.84 = f32[2,16,128,128]{3,2,1,0:T(8,128)} custom-call(bf16[16,256,256]{2,1,0:T(8,128)(2,1)} %get-tuple-element.9.m1_in, bf16[2,512,512]{2,1,0:T(8,128)(2,1)} %get-tuple-element.10.m2_in, f32[2,16,128]{2,1,0:T(8,128)S(1)} %get-tuple-element.11.first, f32[2,128,128]{2,1,0:T(8,128)S(1)} %get-tuple-element.12.second, f32[128,32,128]{2,1,0:T(8,128)S(1)} %all-to-all-done.got), custom_call_target="tpu_custom_call" | custom-call | flops 4194304000 | bytes 10485760 | tf_op jit(solution)/shard_map/pallas_call | solution.py:496
Async XLA Ops:
  3.6 11.2 %copy-start = (f32[2,4]{1,0:T(2,128)S(1)}, f32[2,4]{1,0:T(2,128)}, u32[]{:S(2)}) copy-start(f32[2,4]{1,0:T(2,128)} %deform.3) | copy-start | bytes 100
  3.6 11.2 %copy-start.1 = (f32[256,512]{1,0:T(8,128)S(1)}, f32[256,512]{1,0:T(8,128)}, u32[]{:S(2)}) copy-start(f32[256,512]{1,0:T(8,128)} %constant.14.clone.wide) | copy-start | bytes 1572868
  3.7 11.2 %copy-start.2 = (f32[5,8,1024]{2,1,0:T(8,128)S(1)}, f32[5,8,1024]{2,1,0:T(8,128)}, u32[]{:S(2)}) copy-start(f32[5,8,1024]{2,1,0:T(8,128)} %constant.13.clone.outer) | copy-start | bytes 491524
  3.7 11.2 %copy-start.3 = (f32[5,16,512]{2,1,0:T(8,128)S(1)}, f32[5,16,512]{2,1,0:T(8,128)}, u32[]{:S(2)}) copy-start(f32[5,16,512]{2,1,0:T(8,128)} %constant.12.clone.inner) | copy-start | bytes 491524
  3.7 11.2 %copy-start.4 = (f32[128,256]{1,0:T(8,128)S(1)}, f32[128,256]{1,0:T(8,128)}, u32[]{:S(2)}) copy-start(f32[128,256]{1,0:T(8,128)} %constant.15.clone.px) | copy-start | bytes 393220
  3.7 11.2 %copy-start.5 = (f32[64,128]{1,0:T(8,128)S(1)}, f32[64,128]{1,0:T(8,128)}, u32[]{:S(2)}) copy-start(f32[64,128]{1,0:T(8,128)} %constant.16.clone.py) | copy-start | bytes 98308
  3.7 11.2 %copy-start.6 = (f32[32,64]{1,0:T(8,128)S(1)}, f32[32,64]{1,0:T(8,128)}, u32[]{:S(2)}) copy-start(f32[32,64]{1,0:T(8,128)} %constant.17.clone.px_last) | copy-start | bytes 24580
  3.7 39.8 %all-to-all-start = ((f32[128,32,128]{2,1,0:T(8,128)}), f32[128,32,128]{2,1,0:T(8,128)S(1)}, u32[]{:S(2)}, u32[]{:S(2)}) async-start(f32[128,32,128]{2,1,0:T(8,128)} %bitcast.1), calls=%async_computation | async-start | bytes 4194304 | tf_op jit(solution)/shard_map/all_to_all | solution.py:528
